TPU v7x, 256 devices: a whole 4x4x8 slice. The times are simulated.
256 devices in a mesh: seq: 32 (over x_hi, z, core), head: 8 (over y, x_lo).
Axes of the slice: x: 4 (x_hi: 2, x_lo: 2; x = x_hi * 2 + x_lo), y: 4, z: 8, core: 2. Of those that a mesh axis runs over, the one named last changes fastest.
Arguments:
- queries: bfloat16 [8192, 8192], P(('seq', 'head')), may hold values from -6 to 6
- keys: bfloat16 [8192, 1024], P(('seq', 'head')), may hold values from -6 to 6
- values: bfloat16 [8192, 1024], P(('seq', 'head')), may hold values from -6 to 6
- grad_out: bfloat16 [8192, 8192], P(('seq', 'head')), may hold values from -6 to 6
- doc_blocks: int32 [16], replicated, may hold values from 1 to 8, 64 in all
Outputs:
- attended: bfloat16 [8192, 8192], P('seq', 'head')
- grad_queries: bfloat16 [8192, 8192], P('seq', 'head')
- grad_keys: bfloat16 [8192, 1024], P('seq', 'head')
- grad_values: bfloat16 [8192, 1024], P('seq', 'head')
Inputs may be any that keep to these rules, and one draw needn't show every extreme that they name: `doc_blocks`: the lengths sum to 64; the largest is exactly 8 blocks in every draw.
All inputs are finite; a program needn't handle non-finite values.
Results may differ from a plain program's by a relative error of at most 0.029.
Values may be sent and summed in bfloat16 or wider, within the bound.
No kernel may reach another device: no remote copies, remote signals or barrier semaphores. Data moves between devices by JAX's collectives and lax.ppermute only.
A program may use at most 64 MiB of HBM per device.

v0:
```python
import jax
import jax.numpy as jnp
from jax import lax
from jax.sharding import PartitionSpec as P

SPAN = 4


def passed_along(block, axis, distance):
    devices = range(lax.axis_size(axis))
    route = [(i - distance, i) for i in devices if i - distance in devices]
    return lax.ppermute(block, axis, route)


def segment_of(positions, block_ends):
    counted = jnp.sum((positions[:, None] >= block_ends[None, :]).astype(jnp.int32), axis=1)
    return jnp.where(positions < 0, -1, counted)


def attend(query_rows, key_rows, value_rows, grad_rows, allowed, scale):
    scores = (
        jnp.einsum("rhd,wd->hrw", query_rows, key_rows, preferred_element_type=jnp.float32) * scale
    )
    scores = jnp.where(allowed[None], scores, -1e30)
    highest = jnp.max(scores, axis=2, keepdims=True)
    weights = jnp.exp(scores - highest)
    probs = weights / jnp.sum(weights, axis=2, keepdims=True)
    probs_low = probs.astype(jnp.bfloat16)
    attended = jnp.einsum(
        "hrw,wd->rhd", probs_low, value_rows, preferred_element_type=jnp.float32
    ).astype(jnp.bfloat16)
    grad_probs = jnp.einsum(
        "rhd,wd->hrw", grad_rows, value_rows, preferred_element_type=jnp.float32
    )
    delta = jnp.sum(grad_rows.astype(jnp.float32) * attended.astype(jnp.float32), axis=2)
    grad_scores = (probs * (grad_probs - jnp.transpose(delta)[:, :, None])).astype(jnp.bfloat16)
    grad_query = (
        jnp.einsum("hrw,wd->rhd", grad_scores, key_rows, preferred_element_type=jnp.float32) * scale
    ).astype(jnp.bfloat16)
    grad_key = (
        jnp.einsum("hrw,rhd->wd", grad_scores, query_rows, preferred_element_type=jnp.float32)
        * scale
    )
    grad_value = jnp.einsum("hrw,rhd->wd", probs_low, grad_rows, preferred_element_type=jnp.float32)
    return (attended, grad_query, grad_key, grad_value)


def local(queries, keys, values, grad_out, doc_blocks):
    query_local, key_local, value_local, grad_local = (
        lax.all_to_all(queries, "head", split_axis=1, concat_axis=0, tiled=True),
        lax.all_to_all(keys, "head", split_axis=1, concat_axis=0, tiled=True),
        lax.all_to_all(values, "head", split_axis=1, concat_axis=0, tiled=True),
        lax.all_to_all(grad_out, "head", split_axis=1, concat_axis=0, tiled=True),
    )
    rows = key_local.shape[0]
    width = key_local.shape[1]
    heads = query_local.shape[1] // width
    here = lax.axis_index("seq")
    earlier = []
    current = (key_local, value_local)
    for distance in range(SPAN):
        current = passed_along((current[0], current[1]), "seq", 1)
        earlier.append(current)
    key_window = jnp.concatenate(
        [earlier[place][0] for place in reversed(range(SPAN))] + [key_local], axis=0
    )
    value_window = jnp.concatenate(
        [earlier[place][1] for place in reversed(range(SPAN))] + [value_local], axis=0
    )
    block_ends = jnp.cumsum(doc_blocks) * 128
    query_pos = here * rows + jnp.arange(rows, dtype=jnp.int32)
    key_pos = here * rows - SPAN * rows + jnp.arange((SPAN + 1) * rows, dtype=jnp.int32)
    same_doc = (
        segment_of(query_pos, block_ends)[:, None] == segment_of(key_pos, block_ends)[None, :]
    )
    allowed = same_doc & (key_pos[None, :] <= query_pos[:, None])
    attended, grad_query, grad_key, grad_value = attend(
        query_local.reshape(rows, heads, width),
        key_window,
        value_window,
        grad_local.reshape(rows, heads, width),
        allowed,
        width ** (-0.5),
    )

    def portion(array, distance):
        return array[(SPAN - distance) * rows : (SPAN - distance + 1) * rows]

    total_key = portion(grad_key, SPAN)
    total_value = portion(grad_value, SPAN)
    for distance in reversed(range(SPAN)):
        total_key, total_value = passed_along((total_key, total_value), "seq", -1)
        total_key = total_key + portion(grad_key, distance)
        total_value = total_value + portion(grad_value, distance)
    return (
        attended.reshape(rows, heads * width),
        grad_query.reshape(rows, heads * width),
        total_key.astype(jnp.bfloat16),
        total_value.astype(jnp.bfloat16),
    )


def solution(mesh):
    return jax.shard_map(
        local,
        mesh=mesh,
        in_specs=(
            P(("seq", "head"), None),
            P(("seq", "head"), None),
            P(("seq", "head"), None),
            P(("seq", "head"), None),
            P(),
        ),
        out_specs=(P("seq", "head"), P("seq", "head"), P("seq", "head"), P("seq", "head")),
        check_vma=False,
    )
```

profile of v0, /device:TPU:6, one launch (start us, length us, event | category | flops | bytes accessed | tf_op | source)
XLA Modules:
  0.0 134.3 jit_solution(10378030899399317435)
XLA Ops:
  0.6 0.8 copy-done
  1.5 0.6 copy_bitcast_fusion.2
  2.1 5.9 %all-to-all-start.1 = ((bf16[32,8,128]{2,0,1:T(8,128)(2,1)}), bf16[32,8,128]{2,0,1:T(8,128)(2,1)S(1)}, u32[]{:S(2)}, u32[]{:S(2)}) async-start(bf16[32,8,128]{2,0,1:T(8,128)(2,1)} %copy_bitcast_fusion.2), calls=%async_computation.1 | async-start | bytes 131072 | tf_op jit(solution)/shard_map/all_to_all | solution.py:51
  8.1 0.7 copy.77
  8.8 0.1 multiply_reduce_fusion.1
  8.9 1.5 %copy_bitcast_fusion.3 = bf16[32,8,128]{2,0,1:T(8,128)(2,1)} fusion(bf16[32,1024]{1,0:T(8,128)(2,1)} %param.7), kind=kLoop, calls=%fused_computation.44 | loop fusion | bytes 131072 | tf_op jit(solution)/shard_map/all_to_all | solution.py:52
  10.5 1.9 %copy.120 = bf16[4,8,8,1024]{3,2,0,1:T(8,128)(2,1)} copy(bf16[4,8,8,1024]{3,2,1,0:T(8,128)(2,1)} %bitcast.90) | data formatting | bytes 1048576 | tf_op jit(solution)/shard_map/all_to_all | solution.py:50
  12.4 0.7 all-to-all-done.1
  13.1 5.0 %all-to-all-start = ((bf16[32,8,128]{2,0,1:T(8,128)(2,1)}), bf16[32,8,128]{2,0,1:T(8,128)(2,1)S(1)}, u32[]{:S(2)}, u32[]{:S(2)}) async-start(bf16[32,8,128]{2,0,1:T(8,128)(2,1)} %copy_bitcast_fusion.3), calls=%async_computation | async-start | bytes 131072 | tf_op jit(solution)/shard_map/all_to_all | solution.py:52
  18.1 1.9 %collective-permute-start.4 = (bf16[256,128]{1,0:T(8,128)(2,1)S(1)}, bf16[256,128]{1,0:T(8,128)(2,1)S(1)}, u32[]{:S(2)}, u32[]{:S(2)}) collective-permute-start(bf16[256,128]{1,0:T(8,128)(2,1)S(1)} %bitcast.94), channel_id=1, source_target_pairs={{0,8},{8,16},{16,24},{24,32},{32,40},{40,48},{48,56},{56,64},{64,7... | collective-permute-start | bytes 196616 | tf_op jit(solution)/shard_map/ppermute | solution.py:12
  20.0 3.1 %all-to-all-done = bf16[32,8,128]{2,0,1:T(8,128)(2,1)S(1)} async-done(((bf16[32,8,128]{2,0,1:T(8,128)(2,1)}), bf16[32,8,128]{2,0,1:T(8,128)(2,1)S(1)}, u32[]{:S(2)}, u32[]{:S(2)}) %all-to-all-start) | async-done | bytes 65568 | tf_op jit(solution)/shard_map/all_to_all | solution.py:52
  23.2 4.7 %all-to-all-start.2 = ((bf16[32,8,1024]{2,0,1:T(8,128)(2,1)}), bf16[32,8,1024]{2,0,1:T(8,128)(2,1)S(1)}, u32[]{:S(2)}, u32[]{:S(2)}) async-start(bf16[32,8,1024]{2,0,1:T(8,128)(2,1)} %bitcast.84), calls=%async_computation.2 | async-start | bytes 1048576 | tf_op jit(solution)/shard_map/all_to_all | solution.py:50
  28.0 1.9 %collective-permute-start = (bf16[256,128]{0,1:T(8,128)(2,1)S(1)}, bf16[256,128]{0,1:T(8,128)(2,1)S(1)}, u32[]{:S(2)}, u32[]{:S(2)}) collective-permute-start(bf16[256,128]{0,1:T(8,128)(2,1)S(1)} %copy.75), channel_id=1, source_target_pairs={{0,8},{8,16},{16,24},{24,32},{32,40},{40,48},{48,56},{56,64},{64,7... | collective-permute-start | bytes 196616 | tf_op jit(solution)/shard_map/ppermute | solution.py:12
  29.9 3.9 %collective-permute-start.5 = (bf16[256,128]{1,0:T(8,128)(2,1)S(1)}, bf16[256,128]{1,0:T(8,128)(2,1)S(1)}, u32[]{:S(2)}, u32[]{:S(2)}) collective-permute-start(bf16[256,128]{1,0:T(8,128)(2,1)S(1)} %collective-permute-done.4), channel_id=1, source_target_pairs={{0,8},{8,16},{16,24},{24,32},{32,40},{40,48},{48,56},{56,64},{64,7... | collective-permute-start | bytes 196616 | tf_op jit(solution)/shard_map/ppermute | solution.py:12
  33.9 3.2 %collective-permute-done = bf16[256,128]{0,1:T(8,128)(2,1)S(1)} collective-permute-done((bf16[256,128]{0,1:T(8,128)(2,1)S(1)}, bf16[256,128]{0,1:T(8,128)(2,1)S(1)}, u32[]{:S(2)}, u32[]{:S(2)}) %collective-permute-start) | collective-permute-done | bytes 65568 | tf_op jit(solution)/shard_map/ppermute | solution.py:12
  37.2 1.9 %collective-permute-start.1 = (bf16[256,128]{0,1:T(8,128)(2,1)S(1)}, bf16[256,128]{0,1:T(8,128)(2,1)S(1)}, u32[]{:S(2)}, u32[]{:S(2)}) collective-permute-start(bf16[256,128]{0,1:T(8,128)(2,1)S(1)} %collective-permute-done), channel_id=1, source_target_pairs={{0,8},{8,16},{16,24},{24,32},{32,40},{40,48},{48,56},{56,64},{64,7... | collective-permute-start | bytes 196616 | tf_op jit(solution)/shard_map/ppermute | solution.py:12
  39.1 1.9 %collective-permute-start.6 = (bf16[256,128]{1,0:T(8,128)(2,1)S(1)}, bf16[256,128]{1,0:T(8,128)(2,1)S(1)}, u32[]{:S(2)}, u32[]{:S(2)}) collective-permute-start(bf16[256,128]{1,0:T(8,128)(2,1)S(1)} %collective-permute-done.5), channel_id=1, source_target_pairs={{0,8},{8,16},{16,24},{24,32},{32,40},{40,48},{48,56},{56,64},{64,7... | collective-permute-start | bytes 196616 | tf_op jit(solution)/shard_map/ppermute | solution.py:12
  41.0 5.3 %collective-permute-done.1 = bf16[256,128]{0,1:T(8,128)(2,1)S(1)} collective-permute-done((bf16[256,128]{0,1:T(8,128)(2,1)S(1)}, bf16[256,128]{0,1:T(8,128)(2,1)S(1)}, u32[]{:S(2)}, u32[]{:S(2)}) %collective-permute-start.1) | collective-permute-done | bytes 65568 | tf_op jit(solution)/shard_map/ppermute | solution.py:12
  46.4 1.9 %collective-permute-start.2 = (bf16[256,128]{0,1:T(8,128)(2,1)S(1)}, bf16[256,128]{0,1:T(8,128)(2,1)S(1)}, u32[]{:S(2)}, u32[]{:S(2)}) collective-permute-start(bf16[256,128]{0,1:T(8,128)(2,1)S(1)} %collective-permute-done.1), channel_id=1, source_target_pairs={{0,8},{8,16},{16,24},{24,32},{32,40},{40,48},{48,56},{56,64},{64,7... | collective-permute-start | bytes 196616 | tf_op jit(solution)/shard_map/ppermute | solution.py:12
  48.3 1.9 %collective-permute-start.7 = (bf16[256,128]{1,0:T(8,128)(2,1)S(1)}, bf16[256,128]{1,0:T(8,128)(2,1)S(1)}, u32[]{:S(2)}, u32[]{:S(2)}) collective-permute-start(bf16[256,128]{1,0:T(8,128)(2,1)S(1)} %collective-permute-done.6), channel_id=1, source_target_pairs={{0,8},{8,16},{16,24},{24,32},{32,40},{40,48},{48,56},{56,64},{64,7... | collective-permute-start | bytes 196616 | tf_op jit(solution)/shard_map/ppermute | solution.py:12
  50.2 0.9 compare_and_fusion
  51.1 1.9 %copy.119 = bf16[4,8,8,1024]{3,2,0,1:T(8,128)(2,1)} copy(bf16[4,8,8,1024]{3,2,1,0:T(8,128)(2,1)} %bitcast.91) | data formatting | bytes 1048576 | tf_op jit(solution)/shard_map/all_to_all | solution.py:53
  53.0 2.5 %collective-permute-done.2 = bf16[256,128]{0,1:T(8,128)(2,1)S(1)} collective-permute-done((bf16[256,128]{0,1:T(8,128)(2,1)S(1)}, bf16[256,128]{0,1:T(8,128)(2,1)S(1)}, u32[]{:S(2)}, u32[]{:S(2)}) %collective-permute-start.2) | collective-permute-done | bytes 65568 | tf_op jit(solution)/shard_map/ppermute | solution.py:12
  55.5 1.9 %collective-permute-start.3 = (bf16[256,128]{0,1:T(8,128)(2,1)S(1)}, bf16[256,128]{0,1:T(8,128)(2,1)S(1)}, u32[]{:S(2)}, u32[]{:S(2)}) collective-permute-start(bf16[256,128]{0,1:T(8,128)(2,1)S(1)} %collective-permute-done.2), channel_id=1, source_target_pairs={{0,8},{8,16},{16,24},{24,32},{32,40},{40,48},{48,56},{56,64},{64,7... | collective-permute-start | bytes 196616 | tf_op jit(solution)/shard_map/ppermute | solution.py:12
  57.6 5.7 %all-to-all-start.3 = ((bf16[32,8,1024]{2,0,1:T(8,128)(2,1)}), bf16[32,8,1024]{2,0,1:T(8,128)(2,1)S(1)}, u32[]{:S(2)}, u32[]{:S(2)}) async-start(bf16[32,8,1024]{2,0,1:T(8,128)(2,1)} %bitcast.83), calls=%async_computation.3 | async-start | bytes 1048576 | tf_op jit(solution)/shard_map/all_to_all | solution.py:53
  63.3 1.5 %collective-permute-done.3 = bf16[256,128]{0,1:T(8,128)(2,1)S(1)} collective-permute-done((bf16[256,128]{0,1:T(8,128)(2,1)S(1)}, bf16[256,128]{0,1:T(8,128)(2,1)S(1)}, u32[]{:S(2)}, u32[]{:S(2)}) %collective-permute-start.3) | collective-permute-done | bytes 65568 | tf_op jit(solution)/shard_map/ppermute | solution.py:12
  65.0 5.8 %all-to-all-done.3 = bf16[32,8,1024]{2,0,1:T(8,128)(2,1)S(1)} async-done(((bf16[32,8,1024]{2,0,1:T(8,128)(2,1)}), bf16[32,8,1024]{2,0,1:T(8,128)(2,1)S(1)}, u32[]{:S(2)}, u32[]{:S(2)}) %all-to-all-start.3) | async-done | bytes 524320 | tf_op jit(solution)/shard_map/all_to_all | solution.py:53
  70.9 0.3 copy.85
  71.3 6.2 %fusion.29 = (f32[8,256]{1,0:T(8,128)S(1)}, f32[8,256,1280]{1,2,0:T(8,128)}) fusion(pred[256,1280]{0,1:T(8,128)(4,1)S(1)} %compare_and_fusion, bf16[256,8,128]{2,1,0:T(8,128)(2,1)S(1)} %bitcast.92, bf16[1280,128]{1,0:T(8,128)(2,1)S(1)} %constant_dynamic-update-slice_fusion.5), kind=kOutput, calls=%fused_computation.63 | convolution fusion | flops 681575680 | bytes 11673600 | tf_op jit(solution)/shard_map/sub | solution.py:26
  77.4 4.9 %fusion.7 = bf16[8,256,1280]{1,2,0:T(8,128)(2,1)S(1)} fusion(f32[8,256,1280]{1,2,0:T(8,128)} %get-tuple-element.25, f32[8,256]{1,0:T(8,128)S(1)} %get-tuple-element.24), kind=kLoop, calls=%fused_computation.11 | loop fusion | flops 5242880 | bytes 15736832 | tf_op jit(solution)/shard_map/convert_element_type | solution.py:28
  82.3 1.5 %convolution_bitcast_fusion = f32[1280,128]{1,0:T(8,128)S(1)} fusion(bf16[8,256,1280]{1,2,0:T(8,128)(2,1)S(1)} %fusion.7, bf16[256,8,128]{0,2,1:T(8,128)(2,1)S(1)} %copy.85), kind=kOutput, calls=%fused_computation.12 | convolution fusion | flops 671088640 | bytes 6422528 | tf_op jit(solution)/shard_map/hrw,rhd->wd/dot_general | solution.py:44
  83.9 7.3 %collective-permute-start.12 = (f32[256,128]{1,0:T(8,128)S(1)}, f32[256,128]{1,0:T(8,128)S(1)}, u32[]{:S(2)}, u32[]{:S(2)}) collective-permute-start(f32[256,128]{1,0:T(8,128)S(1)} %slice.45), channel_id=1, source_target_pairs={{8,0},{16,8},{24,16},{32,24},{40,32},{48,40},{56,48},{64,56},{72,6... | collective-permute-start | bytes 393224 | tf_op jit(solution)/shard_map/ppermute | solution.py:12
  91.2 0.9 multiply_reduce_fusion
  92.1 4.9 %fusion.2 = bf16[8,256,1280]{1,2,0:T(8,128)(2,1)S(1)} fusion(bf16[256,8,128]{0,2,1:T(8,128)(2,1)S(1)} %copy.85, f32[8,256]{1,0:T(8,128)S(1)} %bitcast.97, f32[8,256,1280]{1,2,0:T(8,128)} %get-tuple-element.25, f32[8,256]{1,0:T(8,128)S(1)} %get-tuple-element.24, bf16[1280,128]{0,1:T(8,128)(2,1)S(1)} %constant_dynamic-update-slice_fusion), kind=kOutput, calls=%fused_computation.3 | convolution fusion | flops 681574400 | bytes 16596992 | tf_op jit(solution)/shard_map/rhd,wd->hrw/dot_general | solution.py:32
  97.0 1.5 %fusion.8 = f32[1280,128]{1,0:T(8,128)S(1)} fusion(bf16[8,256,1280]{1,2,0:T(8,128)(2,1)S(1)} %fusion.2, bf16[256,8,128]{2,1,0:T(8,128)(2,1)S(1)} %bitcast.93), kind=kOutput, calls=%fused_computation.14 | convolution fusion | flops 671252480 | bytes 6422528 | tf_op jit(solution)/shard_map/hrw,rhd->wd/dot_general | solution.py:41
  98.6 0.9 fusion.11
  99.5 1.9 %collective-permute-start.8 = (f32[256,128]{1,0:T(8,128)S(1)}, f32[256,128]{1,0:T(8,128)S(1)}, u32[]{:S(2)}, u32[]{:S(2)}) collective-permute-start(f32[256,128]{1,0:T(8,128)S(1)} %slice.40), channel_id=1, source_target_pairs={{8,0},{16,8},{24,16},{32,24},{40,32},{48,40},{56,48},{64,56},{72,6... | collective-permute-start | bytes 393224 | tf_op jit(solution)/shard_map/ppermute | solution.py:12
  101.4 1.0 copy.91
  102.4 1.0 copy.90
  103.4 1.9 %collective-permute-start.13 = (f32[256,128]{1,0:T(8,128)S(1)}, f32[256,128]{1,0:T(8,128)S(1)}, u32[]{:S(2)}, u32[]{:S(2)}) collective-permute-start(f32[256,128]{1,0:T(8,128)S(1)} %slice_add_fusion.3), channel_id=1, source_target_pairs={{8,0},{16,8},{24,16},{32,24},{40,32},{48,40},{56,48},{64,56},{72,6... | collective-permute-start | bytes 393224 | tf_op jit(solution)/shard_map/ppermute | solution.py:12
  105.4 5.9 %collective-permute-start.9 = (f32[256,128]{1,0:T(8,128)S(1)}, f32[256,128]{1,0:T(8,128)S(1)}, u32[]{:S(2)}, u32[]{:S(2)}) collective-permute-start(f32[256,128]{1,0:T(8,128)S(1)} %slice_add_fusion.7), channel_id=1, source_target_pairs={{8,0},{16,8},{24,16},{32,24},{40,32},{48,40},{56,48},{64,56},{72,6... | collective-permute-start | bytes 393224 | tf_op jit(solution)/shard_map/ppermute | solution.py:12
  111.4 3.9 %collective-permute-start.14 = (f32[256,128]{1,0:T(8,128)S(1)}, f32[256,128]{1,0:T(8,128)S(1)}, u32[]{:S(2)}, u32[]{:S(2)}) collective-permute-start(f32[256,128]{1,0:T(8,128)S(1)} %slice_add_fusion.2), channel_id=1, source_target_pairs={{8,0},{16,8},{24,16},{32,24},{40,32},{48,40},{56,48},{64,56},{72,6... | collective-permute-start | bytes 393224 | tf_op jit(solution)/shard_map/ppermute | solution.py:12
  115.3 5.9 %collective-permute-start.10 = (f32[256,128]{1,0:T(8,128)S(1)}, f32[256,128]{1,0:T(8,128)S(1)}, u32[]{:S(2)}, u32[]{:S(2)}) collective-permute-start(f32[256,128]{1,0:T(8,128)S(1)} %slice_add_fusion.6), channel_id=1, source_target_pairs={{8,0},{16,8},{24,16},{32,24},{40,32},{48,40},{56,48},{64,56},{72,6... | collective-permute-start | bytes 393224 | tf_op jit(solution)/shard_map/ppermute | solution.py:12
  121.3 3.9 %collective-permute-start.15 = (f32[256,128]{1,0:T(8,128)S(1)}, f32[256,128]{1,0:T(8,128)S(1)}, u32[]{:S(2)}, u32[]{:S(2)}) collective-permute-start(f32[256,128]{1,0:T(8,128)S(1)} %slice_add_fusion.1), channel_id=1, source_target_pairs={{8,0},{16,8},{24,16},{32,24},{40,32},{48,40},{56,48},{64,56},{72,6... | collective-permute-start | bytes 393224 | tf_op jit(solution)/shard_map/ppermute | solution.py:12
  125.2 5.9 %collective-permute-start.11 = (f32[256,128]{1,0:T(8,128)S(1)}, f32[256,128]{1,0:T(8,128)S(1)}, u32[]{:S(2)}, u32[]{:S(2)}) collective-permute-start(f32[256,128]{1,0:T(8,128)S(1)} %slice_add_fusion.5), channel_id=1, source_target_pairs={{8,0},{16,8},{24,16},{32,24},{40,32},{48,40},{56,48},{64,56},{72,6... | collective-permute-start | bytes 393224 | tf_op jit(solution)/shard_map/ppermute | solution.py:12
  131.2 0.7 fusion.25
  131.8 1.8 %collective-permute-done.11 = f32[256,128]{1,0:T(8,128)S(1)} collective-permute-done((f32[256,128]{1,0:T(8,128)S(1)}, f32[256,128]{1,0:T(8,128)S(1)}, u32[]{:S(2)}, u32[]{:S(2)}) %collective-permute-start.11) | collective-permute-done | bytes 131104 | tf_op jit(solution)/shard_map/ppermute | solution.py:12
  133.7 0.6 fusion.26
  (41 shorter events, 0.8 us)
Async XLA Ops:
  0.6 0.8 copy-start
  2.1 11.0 %all-to-all-start.1 = ((bf16[32,8,128]{2,0,1:T(8,128)(2,1)}), bf16[32,8,128]{2,0,1:T(8,128)(2,1)S(1)}, u32[]{:S(2)}, u32[]{:S(2)}) async-start(bf16[32,8,128]{2,0,1:T(8,128)(2,1)} %copy_bitcast_fusion.2), calls=%async_computation.1 | async-start | bytes 131072 | tf_op jit(solution)/shard_map/all_to_all | solution.py:51
  13.1 10.1 %all-to-all-start = ((bf16[32,8,128]{2,0,1:T(8,128)(2,1)}), bf16[32,8,128]{2,0,1:T(8,128)(2,1)S(1)}, u32[]{:S(2)}, u32[]{:S(2)}) async-start(bf16[32,8,128]{2,0,1:T(8,128)(2,1)} %copy_bitcast_fusion.3), calls=%async_computation | async-start | bytes 131072 | tf_op jit(solution)/shard_map/all_to_all | solution.py:52
  18.1 11.8 %collective-permute-start.4 = (bf16[256,128]{1,0:T(8,128)(2,1)S(1)}, bf16[256,128]{1,0:T(8,128)(2,1)S(1)}, u32[]{:S(2)}, u32[]{:S(2)}) collective-permute-start(bf16[256,128]{1,0:T(8,128)(2,1)S(1)} %bitcast.94), channel_id=1, source_target_pairs={{0,8},{8,16},{16,24},{24,32},{32,40},{40,48},{48,56},{56,64},{64,7... | collective-permute-start | bytes 196616 | tf_op jit(solution)/shard_map/ppermute | solution.py:12
  23.2 34.4 %all-to-all-start.2 = ((bf16[32,8,1024]{2,0,1:T(8,128)(2,1)}), bf16[32,8,1024]{2,0,1:T(8,128)(2,1)S(1)}, u32[]{:S(2)}, u32[]{:S(2)}) async-start(bf16[32,8,1024]{2,0,1:T(8,128)(2,1)} %bitcast.84), calls=%async_computation.2 | async-start | bytes 1048576 | tf_op jit(solution)/shard_map/all_to_all | solution.py:50
  28.0 9.2 %collective-permute-start = (bf16[256,128]{0,1:T(8,128)(2,1)S(1)}, bf16[256,128]{0,1:T(8,128)(2,1)S(1)}, u32[]{:S(2)}, u32[]{:S(2)}) collective-permute-start(bf16[256,128]{0,1:T(8,128)(2,1)S(1)} %copy.75), channel_id=1, source_target_pairs={{0,8},{8,16},{16,24},{24,32},{32,40},{40,48},{48,56},{56,64},{64,7... | collective-permute-start | bytes 196616 | tf_op jit(solution)/shard_map/ppermute | solution.py:12
  29.9 9.2 %collective-permute-start.5 = (bf16[256,128]{1,0:T(8,128)(2,1)S(1)}, bf16[256,128]{1,0:T(8,128)(2,1)S(1)}, u32[]{:S(2)}, u32[]{:S(2)}) collective-permute-start(bf16[256,128]{1,0:T(8,128)(2,1)S(1)} %collective-permute-done.4), channel_id=1, source_target_pairs={{0,8},{8,16},{16,24},{24,32},{32,40},{40,48},{48,56},{56,64},{64,7... | collective-permute-start | bytes 196616 | tf_op jit(solution)/shard_map/ppermute | solution.py:12
  37.2 9.2 %collective-permute-start.1 = (bf16[256,128]{0,1:T(8,128)(2,1)S(1)}, bf16[256,128]{0,1:T(8,128)(2,1)S(1)}, u32[]{:S(2)}, u32[]{:S(2)}) collective-permute-start(bf16[256,128]{0,1:T(8,128)(2,1)S(1)} %collective-permute-done), channel_id=1, source_target_pairs={{0,8},{8,16},{16,24},{24,32},{32,40},{40,48},{48,56},{56,64},{64,7... | collective-permute-start | bytes 196616 | tf_op jit(solution)/shard_map/ppermute | solution.py:12
  39.1 9.2 %collective-permute-start.6 = (bf16[256,128]{1,0:T(8,128)(2,1)S(1)}, bf16[256,128]{1,0:T(8,128)(2,1)S(1)}, u32[]{:S(2)}, u32[]{:S(2)}) collective-permute-start(bf16[256,128]{1,0:T(8,128)(2,1)S(1)} %collective-permute-done.5), channel_id=1, source_target_pairs={{0,8},{8,16},{16,24},{24,32},{32,40},{40,48},{48,56},{56,64},{64,7... | collective-permute-start | bytes 196616 | tf_op jit(solution)/shard_map/ppermute | solution.py:12
  46.4 9.2 %collective-permute-start.2 = (bf16[256,128]{0,1:T(8,128)(2,1)S(1)}, bf16[256,128]{0,1:T(8,128)(2,1)S(1)}, u32[]{:S(2)}, u32[]{:S(2)}) collective-permute-start(bf16[256,128]{0,1:T(8,128)(2,1)S(1)} %collective-permute-done.1), channel_id=1, source_target_pairs={{0,8},{8,16},{16,24},{24,32},{32,40},{40,48},{48,56},{56,64},{64,7... | collective-permute-start | bytes 196616 | tf_op jit(solution)/shard_map/ppermute | solution.py:12
  48.3 9.2 %collective-permute-start.7 = (bf16[256,128]{1,0:T(8,128)(2,1)S(1)}, bf16[256,128]{1,0:T(8,128)(2,1)S(1)}, u32[]{:S(2)}, u32[]{:S(2)}) collective-permute-start(bf16[256,128]{1,0:T(8,128)(2,1)S(1)} %collective-permute-done.6), channel_id=1, source_target_pairs={{0,8},{8,16},{16,24},{24,32},{32,40},{40,48},{48,56},{56,64},{64,7... | collective-permute-start | bytes 196616 | tf_op jit(solution)/shard_map/ppermute | solution.py:12
  55.5 9.3 %collective-permute-start.3 = (bf16[256,128]{0,1:T(8,128)(2,1)S(1)}, bf16[256,128]{0,1:T(8,128)(2,1)S(1)}, u32[]{:S(2)}, u32[]{:S(2)}) collective-permute-start(bf16[256,128]{0,1:T(8,128)(2,1)S(1)} %collective-permute-done.2), channel_id=1, source_target_pairs={{0,8},{8,16},{16,24},{24,32},{32,40},{40,48},{48,56},{56,64},{64,7... | collective-permute-start | bytes 196616 | tf_op jit(solution)/shard_map/ppermute | solution.py:12
  57.6 13.3 %all-to-all-start.3 = ((bf16[32,8,1024]{2,0,1:T(8,128)(2,1)}), bf16[32,8,1024]{2,0,1:T(8,128)(2,1)S(1)}, u32[]{:S(2)}, u32[]{:S(2)}) async-start(bf16[32,8,1024]{2,0,1:T(8,128)(2,1)} %bitcast.83), calls=%async_computation.3 | async-start | bytes 1048576 | tf_op jit(solution)/shard_map/all_to_all | solution.py:53
  83.9 19.6 %collective-permute-start.12 = (f32[256,128]{1,0:T(8,128)S(1)}, f32[256,128]{1,0:T(8,128)S(1)}, u32[]{:S(2)}, u32[]{:S(2)}) collective-permute-start(f32[256,128]{1,0:T(8,128)S(1)} %slice.45), channel_id=1, source_target_pairs={{8,0},{16,8},{24,16},{32,24},{40,32},{48,40},{56,48},{64,56},{72,6... | collective-permute-start | bytes 393224 | tf_op jit(solution)/shard_map/ppermute | solution.py:12
  99.5 5.9 %collective-permute-start.8 = (f32[256,128]{1,0:T(8,128)S(1)}, f32[256,128]{1,0:T(8,128)S(1)}, u32[]{:S(2)}, u32[]{:S(2)}) collective-permute-start(f32[256,128]{1,0:T(8,128)S(1)} %slice.40), channel_id=1, source_target_pairs={{8,0},{16,8},{24,16},{32,24},{40,32},{48,40},{56,48},{64,56},{72,6... | collective-permute-start | bytes 393224 | tf_op jit(solution)/shard_map/ppermute | solution.py:12
  103.4 7.9 %collective-permute-start.13 = (f32[256,128]{1,0:T(8,128)S(1)}, f32[256,128]{1,0:T(8,128)S(1)}, u32[]{:S(2)}, u32[]{:S(2)}) collective-permute-start(f32[256,128]{1,0:T(8,128)S(1)} %slice_add_fusion.3), channel_id=1, source_target_pairs={{8,0},{16,8},{24,16},{32,24},{40,32},{48,40},{56,48},{64,56},{72,6... | collective-permute-start | bytes 393224 | tf_op jit(solution)/shard_map/ppermute | solution.py:12
  105.4 9.9 %collective-permute-start.9 = (f32[256,128]{1,0:T(8,128)S(1)}, f32[256,128]{1,0:T(8,128)S(1)}, u32[]{:S(2)}, u32[]{:S(2)}) collective-permute-start(f32[256,128]{1,0:T(8,128)S(1)} %slice_add_fusion.7), channel_id=1, source_target_pairs={{8,0},{16,8},{24,16},{32,24},{40,32},{48,40},{56,48},{64,56},{72,6... | collective-permute-start | bytes 393224 | tf_op jit(solution)/shard_map/ppermute | solution.py:12
  111.4 9.9 %collective-permute-start.14 = (f32[256,128]{1,0:T(8,128)S(1)}, f32[256,128]{1,0:T(8,128)S(1)}, u32[]{:S(2)}, u32[]{:S(2)}) collective-permute-start(f32[256,128]{1,0:T(8,128)S(1)} %slice_add_fusion.2), channel_id=1, source_target_pairs={{8,0},{16,8},{24,16},{32,24},{40,32},{48,40},{56,48},{64,56},{72,6... | collective-permute-start | bytes 393224 | tf_op jit(solution)/shard_map/ppermute | solution.py:12
  115.3 9.9 %collective-permute-start.10 = (f32[256,128]{1,0:T(8,128)S(1)}, f32[256,128]{1,0:T(8,128)S(1)}, u32[]{:S(2)}, u32[]{:S(2)}) collective-permute-start(f32[256,128]{1,0:T(8,128)S(1)} %slice_add_fusion.6), channel_id=1, source_target_pairs={{8,0},{16,8},{24,16},{32,24},{40,32},{48,40},{56,48},{64,56},{72,6... | collective-permute-start | bytes 393224 | tf_op jit(solution)/shard_map/ppermute | solution.py:12
  121.3 9.9 %collective-permute-start.15 = (f32[256,128]{1,0:T(8,128)S(1)}, f32[256,128]{1,0:T(8,128)S(1)}, u32[]{:S(2)}, u32[]{:S(2)}) collective-permute-start(f32[256,128]{1,0:T(8,128)S(1)} %slice_add_fusion.1), channel_id=1, source_target_pairs={{8,0},{16,8},{24,16},{32,24},{40,32},{48,40},{56,48},{64,56},{72,6... | collective-permute-start | bytes 393224 | tf_op jit(solution)/shard_map/ppermute | solution.py:12
  125.2 8.4 %collective-permute-start.11 = (f32[256,128]{1,0:T(8,128)S(1)}, f32[256,128]{1,0:T(8,128)S(1)}, u32[]{:S(2)}, u32[]{:S(2)}) collective-permute-start(f32[256,128]{1,0:T(8,128)S(1)} %slice_add_fusion.5), channel_id=1, source_target_pairs={{8,0},{16,8},{24,16},{32,24},{40,32},{48,40},{56,48},{64,56},{72,6... | collective-permute-start | bytes 393224 | tf_op jit(solution)/shard_map/ppermute | solution.py:12
where the time goes:
time: 135 us; the launch traced here: 134 us
  starting transfers between devices  75.4 us (56%)
  waiting for transfers between devices  24.2 us (18%)
  matrix products  15.9 us (12%)
  local copies, waits for them, and re-layouts  10.2 us (8%)
  other arithmetic  7.52 us (6%)
    ppermute x16, starting transfers between devices, passed_along(): return lax.ppermute(block, axis, route)  54.1 us
    ppermute x16, waiting for transfers between devices, passed_along(): return lax.ppermute(block, axis, route)  14.5 us
    sub x1, matrix products, attend(): weights = jnp.exp(scores - highest)  6.17 us
    all_to_all x1, starting transfers between devices, local(): lax.all_to_all(keys, 'head', split_axis=1, concat_axis=0, tiled=True)  5.93 us
    all_to_all x1, waiting for transfers between devices, local(): lax.all_to_all(grad_out, 'head', split_axis=1, concat_axis=0, tiled=True)  5.84 us
    all_to_all x1, starting transfers between devices, local(): lax.all_to_all(grad_out, 'head', split_axis=1, concat_axis=0, tiled=True)  5.74 us
    all_to_all x1, starting transfers between devices, local(): lax.all_to_all(values, 'head', split_axis=1, concat_axis=0, tiled=True)  5 us
    dot_general x1, matrix products, attend(): jnp.einsum('rhd,wd->hrw', grad_rows, value_rows, preferred_element_type=j...  4.95 us
  transfers between devices with their start and end apart: 20, of which 8 were waited for; matrix products, arithmetic and copies ran while one was open for 14% of the time, Pallas kernels for 0%

commit v1 on v0

v1 whole, which is shorter than its diff:
```python
import jax
import jax.numpy as jnp
from jax import lax
from jax.experimental import pallas as pl
from jax.experimental.pallas import tpu as pltpu
from jax.sharding import PartitionSpec as P

HD = 128
BLOCK = 128
HEADS = 8
ROWS = 256
SCALE = HD**-0.5
EXP2_SCALE = SCALE * 1.4426950408889634
WINDOW = 9
REACH = 8


def document_start(doc_ref, block):
    end = jnp.int32(0)
    start = jnp.int32(0)
    for doc in range(doc_ref.shape[0]):
        start = jnp.where(end <= block, end, start)
        end = end + doc_ref[doc]
    return start


def attention_kernel(
    doc_ref, qg_ref, mine_ref, theirs_ref,
    att_ref, gq_ref, kept_ref, sent_ref,
    kw, vw, kt, vt, dk, dv,
):
    here = lax.axis_index("seq")
    parity = lax.rem(here, 2)
    far = pl.multiple_of(512 - 256 * parity, 128)
    near = pl.multiple_of(256 - 256 * parity, 128)
    for part, (window, turned) in enumerate(((kw, kt), (vw, vt))):
        at = part * HD
        window[0:128, :] = mine_ref[128:256, 512 + at : 512 + at + HD]
        window[128:384, :] = theirs_ref[:, pl.ds(far + at, HD)]
        window[384:640, :] = mine_ref[:, 256 + at : 256 + at + HD]
        window[640:896, :] = theirs_ref[:, pl.ds(near + at, HD)]
        window[896:1152, :] = mine_ref[:, at : at + HD]
        turned[...] = window[...].T
    dk[...] = jnp.zeros_like(dk)
    dv[...] = jnp.zeros_like(dv)

    starts = [document_start(doc_ref, 2 * here + half) for half in range(2)]
    key_at = lax.broadcasted_iota(jnp.int32, (BLOCK, 2 * BLOCK), 0)
    query_at = lax.rem(lax.broadcasted_iota(jnp.int32, (BLOCK, 2 * BLOCK), 1), BLOCK)
    causal = key_at <= query_at

    def stacked(ref, half, column):
        rows = pl.ds(half * BLOCK, BLOCK)
        return jnp.concatenate(
            [ref[rows, pl.ds(pl.multiple_of(column + i * HD, HD), HD)] for i in range(2)], axis=0
        )

    def pair_of_heads(pair, _):
        column = pair * (2 * HD)
        for half in range(2):
            low, high = half * BLOCK, (half + REACH) * BLOCK
            valid = [
                2 * here - 7 + half + w >= starts[half] for w in range(REACH - 1)
            ]
            q2 = stacked(qg_ref, half, column)
            g2 = stacked(qg_ref, half, HEADS * HD + column)
            qt, gt = q2.T, g2.T
            scores = jnp.dot(kw[low:high, :], qt, preferred_element_type=jnp.float32)
            pieces = [scores[w * BLOCK : (w + 1) * BLOCK, :] for w in range(REACH)]
            pieces[-1] = jnp.where(causal, pieces[-1], -1e30)
            highest = jnp.max(pieces[-1], axis=0, keepdims=True)
            for w in range(REACH - 1):
                top = jnp.max(pieces[w], axis=0, keepdims=True)
                highest = jnp.maximum(highest, jnp.where(valid[w], top, -1e30))
            shift = highest * EXP2_SCALE
            weights = [
                jnp.exp2(
                    piece * EXP2_SCALE
                    - (shift if w == REACH - 1 else jnp.where(valid[w], shift, 1e30))
                )
                for w, piece in enumerate(pieces)
            ]
            weights = jnp.concatenate(weights, axis=0)
            total = jnp.sum(weights, axis=0, keepdims=True)
            probs = weights * (1.0 / total)
            probs_low = probs.astype(jnp.bfloat16)
            att_t = jnp.dot(
                vt[:, low:high], probs_low, preferred_element_type=jnp.float32
            ).astype(jnp.bfloat16)
            delta = jnp.sum(
                gt.astype(jnp.float32) * att_t.astype(jnp.float32), axis=0, keepdims=True
            )
            grad_probs = jnp.dot(vw[low:high, :], gt, preferred_element_type=jnp.float32)
            grad_scores = (probs * (grad_probs - delta)).astype(jnp.bfloat16)
            gq_t = (
                jnp.dot(kt[:, low:high], grad_scores, preferred_element_type=jnp.float32) * SCALE
            ).astype(jnp.bfloat16)
            dv[low:high, :] += jnp.dot(probs_low, g2, preferred_element_type=jnp.float32)
            dk[low:high, :] += jnp.dot(grad_scores, q2, preferred_element_type=jnp.float32)
            rows = pl.ds(half * BLOCK, BLOCK)
            for i in range(2):
                columns = pl.ds(pl.multiple_of(column + i * HD, HD), HD)
                att_ref[rows, columns] = att_t[:, i * BLOCK : (i + 1) * BLOCK].T
                gq_ref[rows, columns] = gq_t[:, i * BLOCK : (i + 1) * BLOCK].T
        return 0

    lax.fori_loop(0, HEADS // 2, pair_of_heads, 0)

    for part, (total, factor) in enumerate(((dk, SCALE), (dv, None))):
        scaled = total[...] if factor is None else total[...] * factor
        at = part * HD
        kept_ref[:, at : at + HD] = scaled[896:1152, :]
        kept_ref[:, 256 + at : 256 + at + HD] = scaled[384:640, :]
        kept_ref[0:128, 512 + at : 512 + at + HD] = jnp.zeros((128, HD), jnp.float32)
        kept_ref[128:256, 512 + at : 512 + at + HD] = scaled[0:128, :]
        sent_ref[:, at : at + HD] = scaled[640:896, :].astype(jnp.bfloat16)
        sent_ref[:, 256 + at : 256 + at + HD] = scaled[128:384, :].astype(jnp.bfloat16)


def attention(doc_blocks, qg, mine, theirs):
    vmem = pl.BlockSpec(memory_space=pltpu.VMEM)
    window = WINDOW * BLOCK
    return pl.pallas_call(
        attention_kernel,
        out_shape=(
            jax.ShapeDtypeStruct((ROWS, HEADS * HD), jnp.bfloat16),
            jax.ShapeDtypeStruct((ROWS, HEADS * HD), jnp.bfloat16),
            jax.ShapeDtypeStruct((ROWS, 6 * HD), jnp.float32),
            jax.ShapeDtypeStruct((ROWS, 4 * HD), jnp.bfloat16),
        ),
        in_specs=[pl.BlockSpec(memory_space=pltpu.SMEM), vmem, vmem, vmem],
        out_specs=(vmem, vmem, vmem, vmem),
        scratch_shapes=[
            pltpu.VMEM((window, HD), jnp.bfloat16),
            pltpu.VMEM((window, HD), jnp.bfloat16),
            pltpu.VMEM((HD, window), jnp.bfloat16),
            pltpu.VMEM((HD, window), jnp.bfloat16),
            pltpu.VMEM((window, HD), jnp.float32),
            pltpu.VMEM((window, HD), jnp.float32),
        ],
        compiler_params=pltpu.CompilerParams(vmem_limit_bytes=40 * 1024 * 1024),
        cost_estimate=pl.CostEstimate(
            flops=3_000_000_000, bytes_accessed=4_000_000, transcendentals=2_100_000
        ),
    )(doc_blocks, qg, mine, theirs)


def shifted(block, distance):
    devices = range(lax.axis_size("seq"))
    route = [(i - distance, i) for i in devices if i - distance in devices]
    return lax.ppermute(block, "seq", route)


def partners(block):
    return lax.ppermute(block, "seq", [(i, i ^ 1) for i in range(lax.axis_size("seq"))])


def by_group(array):
    groups = lax.axis_size("head")
    rows, columns = array.shape
    return jnp.transpose(array.reshape(rows, groups, columns // groups), (1, 0, 2))


def to_groups(chunks):
    received = lax.all_to_all(chunks, "head", split_axis=0, concat_axis=0, tiled=True)
    return received.reshape(-1, chunks.shape[2])


def local(queries, keys, values, grad_out, doc_blocks):
    keys_values = jnp.concatenate([keys, values], axis=1)
    two_back = shifted(keys_values, 2)
    four_back = shifted(keys_values, 4)
    qg = to_groups(jnp.concatenate([by_group(queries), by_group(grad_out)], axis=2))
    width = keys.shape[1]
    mine = to_groups(
        jnp.concatenate(
            [
                by_group(array[:, at : at + width])
                for array in (keys_values, two_back, four_back)
                for at in (0, width)
            ],
            axis=2,
        )
    )
    theirs = partners(mine)
    attended, grad_queries, kept, sent = attention(doc_blocks, qg, mine, theirs)
    odd = lax.rem(lax.axis_index("seq"), 2) == 1
    swapped = partners(sent).astype(jnp.float32)
    one, three = swapped[:, 0:256], swapped[:, 256:512]
    for_here = kept[:, 0:256] + jnp.where(odd, 0.0, one)
    for_two = (kept[:, 256:512] + jnp.where(odd, one, three)).astype(jnp.bfloat16)
    for_four = (kept[:, 512:768] + jnp.where(odd, three, 0.0)).astype(jnp.bfloat16)
    total = (
        for_here
        + shifted(for_two, -2).astype(jnp.float32)
        + shifted(for_four, -4).astype(jnp.float32)
    ).astype(jnp.bfloat16)
    return attended, grad_queries, total[:, 0:128], total[:, 128:256]


def solution(mesh):
    rows = P(("seq", "head"), None)
    return jax.shard_map(
        local,
        mesh=mesh,
        in_specs=(rows, rows, rows, rows, P()),
        out_specs=(P("seq", "head"),) * 4,
        check_vma=False,
    )
```

time: 135 us -> 84 us (0.62)
  starting transfers between devices: 75.4 us -> 29.1 us
  matrix products: 15.9 us -> 0 us
  Pallas kernels: 0 us -> 14.7 us
  other arithmetic: 7.52 us -> 1.27 us
  waiting for transfers between devices: 24.2 us -> 29.2 us
  local copies, waits for them, and re-layouts: 10.2 us -> 8.01 us
    ppermute x16 -> x6, starting transfers between devices: 54.1 us -> 18.5 us  [the longest x4 18.5 us: shifted(): return lax.ppermute(block, 'seq', route)]
    pallas_call x0 -> x1, Pallas kernels: none -> 14.7 us  [attention(): pl.pallas_call(attention_kernel, out_shape=(jax.ShapeDtypeStruct((ROWS, H...]
    all_to_all x4 -> x2, starting transfers between devices: 21.3 us -> 10.6 us  [to_groups(): lax.all_to_all(chunks, 'head', split_axis=0, concat_axis=0, tiled=True)]
    dot_general x5 -> x0, matrix products: 9.76 us -> none  [the longest x1 4.95 us: attend(): jnp.einsum('rhd,wd->hrw', grad_rows, value_rows, preferred_element_type=j...]
    all_to_all x4 -> x2, waiting for transfers between devices: 9.69 us -> 16.1 us  [to_groups(): lax.all_to_all(chunks, 'head', split_axis=0, concat_axis=0, tiled=True)]
    sub x1 -> x0, matrix products: 6.17 us -> none  [attend(): weights = jnp.exp(scores - highest)]
    all_to_all x5 -> x0, local copies, waits for them, and re-layouts: 5.98 us -> none  [the longest x1 1.88 us: local(): lax.all_to_all(queries, 'head', split_axis=1, concat_axis=0, tiled=True)]
    convert_element_type x3, other arithmetic: 6.17 us -> 0.2 us  [the longest x1 0.08 us: local(): (kept[:, 256:512] + jnp.where(odd, one, three)).astype(jnp.bfloat16)]
  transfers between devices with their start and end apart: 20 -> 8, of which waited for: 8 -> 7; matrix products, arithmetic and copies ran while one was open for 14% -> 7% of each run, Pallas kernels for 0% -> 0%
where the time goes in v1:
time: 84 us; the launch traced here: 83 us
  waiting for transfers between devices  29.2 us (35%)
  starting transfers between devices  29.1 us (35%)
  Pallas kernels  14.7 us (18%)
  local copies, waits for them, and re-layouts  8.01 us (10%)
  other arithmetic  1.27 us (2%)
    ppermute x4, starting transfers between devices, shifted(): return lax.ppermute(block, 'seq', route)  18.5 us
    all_to_all x2, waiting for transfers between devices, to_groups(): lax.all_to_all(chunks, 'head', split_axis=0, concat_axis=0, tiled=True)  16.1 us
    pallas_call x1, Pallas kernels, attention(): pl.pallas_call(attention_kernel, out_shape=(jax.ShapeDtypeStruct((ROWS, H...  14.7 us
    all_to_all x2, starting transfers between devices, to_groups(): lax.all_to_all(chunks, 'head', split_axis=0, concat_axis=0, tiled=True)  10.6 us
    ppermute x4, waiting for transfers between devices, shifted(): return lax.ppermute(block, 'seq', route)  9.84 us
    unnamed x14, local copies, waits for them, and re-layouts  5.77 us
    ppermute x2, waiting for transfers between devices, partners(): lax.ppermute(block, 'seq', [(i, i ^ 1) for i in range(lax.axis_size('seq'...  3.25 us
  transfers between devices with their start and end apart: 8, of which 7 were waited for; matrix products, arithmetic and copies ran while one was open for 7% of the time, Pallas kernels for 0%

profile of v1, /device:TPU:6, one launch (start us, length us, event | category | flops | bytes accessed | tf_op | source)
XLA Modules:
  0.0 83.0 jit_solution(8813358661254541985)
XLA Ops:
  0.6 0.8 %constant_dynamic-update-slice_fusion.1 = bf16[32,2048]{1,0:T(8,128)(2,1)S(1)} fusion(bf16[32,1024]{1,0:T(8,128)(2,1)} %param.6), kind=kLoop, calls=%fused_computation.23 | loop fusion | bytes 131072
  1.5 0.8 %constant_dynamic-update-slice_fusion = bf16[32,2048]{1,0:T(8,128)(2,1)S(1)} fusion(bf16[32,2048]{1,0:T(8,128)(2,1)S(1)} %constant_dynamic-update-slice_fusion.1, bf16[32,1024]{1,0:T(8,128)(2,1)} %param.7), kind=kLoop, calls=%fused_computation.22 | loop fusion | bytes 131072 | tf_op jit(solution)/shard_map/concatenate | solution.py:170
  2.3 0.0 copy-start.1
  2.3 0.0 copy-start.2
  2.3 4.0 %collective-permute-start = (bf16[32,2048]{1,0:T(8,128)(2,1)S(1)}, bf16[32,2048]{1,0:T(8,128)(2,1)S(1)}, u32[]{:S(2)}, u32[]{:S(2)}) collective-permute-start(bf16[32,2048]{1,0:T(8,128)(2,1)S(1)} %constant_dynamic-update-slice_fusion), channel_id=1, source_target_pairs={{0,16},{8,24},{16,32},{24,40},{32,48},{40,56},{48,64},{56,72},{64,... | collective-permute-start | bytes 393224 | tf_op jit(solution)/shard_map/ppermute | solution.py:151
  6.3 5.2 %collective-permute-start.1 = (bf16[32,2048]{1,0:T(8,128)(2,1)S(1)}, bf16[32,2048]{1,0:T(8,128)(2,1)S(1)}, u32[]{:S(2)}, u32[]{:S(2)}) collective-permute-start(bf16[32,2048]{1,0:T(8,128)(2,1)S(1)} %constant_dynamic-update-slice_fusion), channel_id=1, source_target_pairs={{0,32},{8,40},{16,48},{24,56},{32,64},{40,72},{48,80},{56,88},{64,... | collective-permute-start | bytes 393224 | tf_op jit(solution)/shard_map/ppermute | solution.py:151
  11.5 1.5 %fusion.5 = bf16[8,32,768]{2,1,0:T(8,128)(2,1)} fusion(bf16[32,1024]{1,0:T(8,128)(2,1)} %param.6), kind=kLoop, calls=%fused_computation.17 | loop fusion | bytes 131072
  13.0 1.5 %fusion.4 = bf16[8,32,768]{2,1,0:T(8,128)(2,1)} fusion(bf16[8,32,768]{2,1,0:T(8,128)(2,1)} %fusion.5, bf16[32,1024]{1,0:T(8,128)(2,1)} %param.7), kind=kLoop, calls=%fused_computation.15 | loop fusion | bytes 131072
  14.4 0.1 collective-permute-done
  14.6 0.6 fusion.3
  15.2 0.6 fusion.2
  15.9 4.2 %collective-permute-done.1 = bf16[32,2048]{1,0:T(8,128)(2,1)S(1)} collective-permute-done((bf16[32,2048]{1,0:T(8,128)(2,1)S(1)}, bf16[32,2048]{1,0:T(8,128)(2,1)S(1)}, u32[]{:S(2)}, u32[]{:S(2)}) %collective-permute-start.1) | collective-permute-done | bytes 131104 | tf_op jit(solution)/shard_map/ppermute | solution.py:151
  20.0 0.6 fusion.1
  20.7 0.6 fusion
  21.3 5.9 %all-to-all-start.1 = ((bf16[8,32,768]{2,1,0:T(8,128)(2,1)}), bf16[8,32,768]{2,1,0:T(8,128)(2,1)S(1)}, u32[]{:S(2)}, u32[]{:S(2)}) async-start(bf16[8,32,768]{2,1,0:T(8,128)(2,1)} %fusion), calls=%async_computation.1 | async-start | bytes 786432 | tf_op jit(solution)/shard_map/all_to_all | solution.py:165
  27.2 0.0 copy-done.1
  27.2 0.0 copy-done.2
  27.2 0.1 bitcast_bitcast_fusion
  27.3 1.1 %pad_maximum_fusion = bf16[8,32,2048]{2,1,0:T(8,128)(2,1)} fusion(bf16[8,32,1024]{2,1,0:T(8,128)(2,1)S(1)} %get-tuple-element.20, bf16[8,32,1024]{2,1,0:T(8,128)(2,1)S(1)} %get-tuple-element.21), kind=kLoop, calls=%fused_computation | loop fusion | flops 2097152 | bytes 2097152 | tf_op jit(solution)/shard_map/concatenate | solution.py:173
  28.4 0.0 copy-start
  28.4 5.6 %all-to-all-done.1 = bf16[8,32,768]{2,1,0:T(8,128)(2,1)S(1)} async-done(((bf16[8,32,768]{2,1,0:T(8,128)(2,1)}), bf16[8,32,768]{2,1,0:T(8,128)(2,1)S(1)}, u32[]{:S(2)}, u32[]{:S(2)}) %all-to-all-start.1) | async-done | bytes 393248 | tf_op jit(solution)/shard_map/all_to_all | solution.py:165
  34.1 4.6 %all-to-all-start = ((bf16[8,32,2048]{2,1,0:T(8,128)(2,1)}), bf16[8,32,2048]{2,1,0:T(8,128)(2,1)S(1)}, u32[]{:S(2)}, u32[]{:S(2)}) async-start(bf16[8,32,2048]{2,1,0:T(8,128)(2,1)} %pad_maximum_fusion), calls=%async_computation | async-start | bytes 2097152 | tf_op jit(solution)/shard_map/all_to_all | solution.py:165
  38.7 0.0 collective-permute-start.2
  38.7 1.7 %collective-permute-done.2.theirs_ref = bf16[256,768]{1,0:T(8,128)(2,1)S(1)} collective-permute-done((bf16[256,768]{1,0:T(8,128)(2,1)S(1)}, bf16[256,768]{1,0:T(8,128)(2,1)S(1)}, u32[]{:S(2)}, u32[]{:S(2)}) %collective-permute-start.2) | collective-permute-done | bytes 393248 | tf_op jit(solution)/shard_map/ppermute | solution.py:155
  40.4 10.5 %all-to-all-done = bf16[8,32,2048]{2,1,0:T(8,128)(2,1)S(1)} async-done(((bf16[8,32,2048]{2,1,0:T(8,128)(2,1)}), bf16[8,32,2048]{2,1,0:T(8,128)(2,1)S(1)}, u32[]{:S(2)}, u32[]{:S(2)}) %all-to-all-start) | async-done | bytes 1048608 | tf_op jit(solution)/shard_map/all_to_all | solution.py:165
  50.9 0.0 copy-done
  50.9 14.7 %shard_map.84 = (bf16[256,1024]{1,0:T(8,128)(2,1)}, bf16[256,1024]{1,0:T(8,128)(2,1)}, f32[256,768]{1,0:T(8,128)S(1)}, bf16[256,512]{1,0:T(8,128)(2,1)S(1)}) custom-call(s32[16]{0:T(128)S(1)} %copy-done, bf16[256,2048]{1,0:T(8,128)(2,1)S(1)} %bitcast.74, bf16[256,768]{1,0:T(8,128)(2,1)S(1)} %bitcast.76, bf16[256,768]{1,0:T(8,128)(2,1)S(1)} %collective-permute-done.2.theirs_ref), custom_call_target="tpu_custom_call" | custom-call | flops 3000000000 | bytes 4000000 | tf_op jit(solution)/shard_map/pallas_call | solution.py:123
  65.6 0.0 collective-permute-start.3
  65.6 1.5 %collective-permute-done.3 = bf16[256,512]{1,0:T(8,128)(2,1)S(1)} collective-permute-done((bf16[256,512]{1,0:T(8,128)(2,1)S(1)}, bf16[256,512]{1,0:T(8,128)(2,1)S(1)}, u32[]{:S(2)}, u32[]{:S(2)}) %collective-permute-start.3) | collective-permute-done | bytes 262176 | tf_op jit(solution)/shard_map/ppermute | solution.py:155
  67.2 0.1 add_convert_fusion.2
  67.3 5.5 %collective-permute-start.4 = (bf16[256,256]{1,0:T(8,128)(2,1)S(1)}, bf16[256,256]{1,0:T(8,128)(2,1)S(1)}, u32[]{:S(2)}, u32[]{:S(2)}) collective-permute-start(bf16[256,256]{1,0:T(8,128)(2,1)S(1)} %get-tuple-element.12), channel_id=1, source_target_pairs={{16,0},{24,8},{32,16},{40,24},{48,32},{56,40},{64,48},{72,56},{80,... | collective-permute-start | bytes 393224 | tf_op jit(solution)/shard_map/ppermute | solution.py:151
  72.7 3.9 %collective-permute-start.5 = (bf16[256,256]{1,0:T(8,128)(2,1)S(1)}, bf16[256,256]{1,0:T(8,128)(2,1)S(1)}, u32[]{:S(2)}, u32[]{:S(2)}) collective-permute-start(bf16[256,256]{1,0:T(8,128)(2,1)S(1)} %get-tuple-element.13), channel_id=1, source_target_pairs={{32,0},{40,8},{48,16},{56,24},{64,32},{72,40},{80,48},{88,56},{96,... | collective-permute-start | bytes 393224 | tf_op jit(solution)/shard_map/ppermute | solution.py:151
  76.7 0.0 collective-permute-done.4
  76.7 5.6 %collective-permute-done.5 = bf16[256,256]{1,0:T(8,128)(2,1)S(1)} collective-permute-done((bf16[256,256]{1,0:T(8,128)(2,1)S(1)}, bf16[256,256]{1,0:T(8,128)(2,1)S(1)}, u32[]{:S(2)}, u32[]{:S(2)}) %collective-permute-start.5) | collective-permute-done | bytes 131104 | tf_op jit(solution)/shard_map/ppermute | solution.py:151
  82.2 0.1 add_convert_fusion
  82.3 0.7 fusion.6
  (3 shorter events, 0.1 us)
Async XLA Ops:
  2.3 24.9 %copy-start.1 = (bf16[32,8192]{1,0:T(8,128)(2,1)S(1)}, bf16[32,8192]{1,0:T(8,128)(2,1)}, u32[]{:S(2)}) copy-start(bf16[32,8192]{1,0:T(8,128)(2,1)} %param.8) | copy-start | bytes 1572868
  2.3 24.9 %copy-start.2 = (bf16[32,8192]{1,0:T(8,128)(2,1)S(1)}, bf16[32,8192]{1,0:T(8,128)(2,1)}, u32[]{:S(2)}) copy-start(bf16[32,8192]{1,0:T(8,128)(2,1)} %param.5) | copy-start | bytes 1572868
  2.3 12.2 %collective-permute-start = (bf16[32,2048]{1,0:T(8,128)(2,1)S(1)}, bf16[32,2048]{1,0:T(8,128)(2,1)S(1)}, u32[]{:S(2)}, u32[]{:S(2)}) collective-permute-start(bf16[32,2048]{1,0:T(8,128)(2,1)S(1)} %constant_dynamic-update-slice_fusion), channel_id=1, source_target_pairs={{0,16},{8,24},{16,32},{24,40},{32,48},{40,56},{48,64},{56,72},{64,... | collective-permute-start | bytes 393224 | tf_op jit(solution)/shard_map/ppermute | solution.py:151
  6.3 13.7 %collective-permute-start.1 = (bf16[32,2048]{1,0:T(8,128)(2,1)S(1)}, bf16[32,2048]{1,0:T(8,128)(2,1)S(1)}, u32[]{:S(2)}, u32[]{:S(2)}) collective-permute-start(bf16[32,2048]{1,0:T(8,128)(2,1)S(1)} %constant_dynamic-update-slice_fusion), channel_id=1, source_target_pairs={{0,32},{8,40},{16,48},{24,56},{32,64},{40,72},{48,80},{56,88},{64,... | collective-permute-start | bytes 393224 | tf_op jit(solution)/shard_map/ppermute | solution.py:151
  21.3 12.8 %all-to-all-start.1 = ((bf16[8,32,768]{2,1,0:T(8,128)(2,1)}), bf16[8,32,768]{2,1,0:T(8,128)(2,1)S(1)}, u32[]{:S(2)}, u32[]{:S(2)}) async-start(bf16[8,32,768]{2,1,0:T(8,128)(2,1)} %fusion), calls=%async_computation.1 | async-start | bytes 786432 | tf_op jit(solution)/shard_map/all_to_all | solution.py:165
  28.4 22.5 %copy-start = (s32[16]{0:T(128)S(1)}, s32[16]{0:T(128)}, u32[]{:S(2)}) copy-start(s32[16]{0:T(128)} %doc_ref.1) | copy-start | bytes 196
  34.1 16.9 %all-to-all-start = ((bf16[8,32,2048]{2,1,0:T(8,128)(2,1)}), bf16[8,32,2048]{2,1,0:T(8,128)(2,1)S(1)}, u32[]{:S(2)}, u32[]{:S(2)}) async-start(bf16[8,32,2048]{2,1,0:T(8,128)(2,1)} %pad_maximum_fusion), calls=%async_computation | async-start | bytes 2097152 | tf_op jit(solution)/shard_map/all_to_all | solution.py:165
  38.7 1.7 %collective-permute-start.2 = (bf16[256,768]{1,0:T(8,128)(2,1)S(1)}, bf16[256,768]{1,0:T(8,128)(2,1)S(1)}, u32[]{:S(2)}, u32[]{:S(2)}) collective-permute-start(bf16[256,768]{1,0:T(8,128)(2,1)S(1)} %bitcast.75), channel_id=1, source_target_pairs={{0,8},{8,0},{16,24},{24,16},{32,40},{40,32},{48,56},{56,48},{64,72... | collective-permute-start | bytes 1179656 | tf_op jit(solution)/shard_map/ppermute | solution.py:155
  65.6 1.5 %collective-permute-start.3 = (bf16[256,512]{1,0:T(8,128)(2,1)S(1)}, bf16[256,512]{1,0:T(8,128)(2,1)S(1)}, u32[]{:S(2)}, u32[]{:S(2)}) collective-permute-start(bf16[256,512]{1,0:T(8,128)(2,1)S(1)} %get-tuple-element.11), channel_id=1, source_target_pairs={{0,8},{8,0},{16,24},{24,16},{32,40},{40,32},{48,56},{56,48},{64,72... | collective-permute-start | bytes 786440 | tf_op jit(solution)/shard_map/ppermute | solution.py:155
  67.3 9.4 %collective-permute-start.4 = (bf16[256,256]{1,0:T(8,128)(2,1)S(1)}, bf16[256,256]{1,0:T(8,128)(2,1)S(1)}, u32[]{:S(2)}, u32[]{:S(2)}) collective-permute-start(bf16[256,256]{1,0:T(8,128)(2,1)S(1)} %get-tuple-element.12), channel_id=1, source_target_pairs={{16,0},{24,8},{32,16},{40,24},{48,32},{56,40},{64,48},{72,56},{80,... | collective-permute-start | bytes 393224 | tf_op jit(solution)/shard_map/ppermute | solution.py:151
  72.7 9.5 %collective-permute-start.5 = (bf16[256,256]{1,0:T(8,128)(2,1)S(1)}, bf16[256,256]{1,0:T(8,128)(2,1)S(1)}, u32[]{:S(2)}, u32[]{:S(2)}) collective-permute-start(bf16[256,256]{1,0:T(8,128)(2,1)S(1)} %get-tuple-element.13), channel_id=1, source_target_pairs={{32,0},{40,8},{48,16},{56,24},{64,32},{72,40},{80,48},{88,56},{96,... | collective-permute-start | bytes 393224 | tf_op jit(solution)/shard_map/ppermute | solution.py:151

commit v2 on v1

--- a/solution.py
+++ b/solution.py
@@ -27,7 +27,7 @@
 def attention_kernel(
     doc_ref, qg_ref, mine_ref, theirs_ref,
     att_ref, gq_ref, kept_ref, sent_ref,
-    kw, vw, kt, vt, dk, dv,
+    kw, vw, kt, vt, dk, dv, scores, weights, grads, qs, gs,
 ):
     here = lax.axis_index("seq")
     parity = lax.rem(here, 2)
@@ -41,9 +41,6 @@
         window[640:896, :] = theirs_ref[:, pl.ds(near + at, HD)]
         window[896:1152, :] = mine_ref[:, at : at + HD]
         turned[...] = window[...].T
-    dk[...] = jnp.zeros_like(dk)
-    dv[...] = jnp.zeros_like(dv)
-
     starts = [document_start(doc_ref, 2 * here + half) for half in range(2)]
     key_at = lax.broadcasted_iota(jnp.int32, (BLOCK, 2 * BLOCK), 0)
     query_at = lax.rem(lax.broadcasted_iota(jnp.int32, (BLOCK, 2 * BLOCK), 1), BLOCK)
@@ -52,59 +49,85 @@
     def stacked(ref, half, column):
         rows = pl.ds(half * BLOCK, BLOCK)
         return jnp.concatenate(
-            [ref[rows, pl.ds(pl.multiple_of(column + i * HD, HD), HD)] for i in range(2)], axis=0
+            [ref[rows, pl.ds(column + i * HD, HD)] for i in range(2)], axis=0
         )
 
-    def pair_of_heads(pair, _):
+    def over_sublanes(op, array):
+        return op(array.reshape(BLOCK // 8, 8, 2 * BLOCK), axis=0)
+
+    def pair_of_heads(pair):
         column = pair * (2 * HD)
         for half in range(2):
             low, high = half * BLOCK, (half + REACH) * BLOCK
-            valid = [
-                2 * here - 7 + half + w >= starts[half] for w in range(REACH - 1)
-            ]
+            valid = [2 * here - 7 + half + w >= starts[half] for w in range(REACH - 1)]
             q2 = stacked(qg_ref, half, column)
             g2 = stacked(qg_ref, half, HEADS * HD + column)
             qt, gt = q2.T, g2.T
-            scores = jnp.dot(kw[low:high, :], qt, preferred_element_type=jnp.float32)
-            pieces = [scores[w * BLOCK : (w + 1) * BLOCK, :] for w in range(REACH)]
-            pieces[-1] = jnp.where(causal, pieces[-1], -1e30)
-            highest = jnp.max(pieces[-1], axis=0, keepdims=True)
-            for w in range(REACH - 1):
-                top = jnp.max(pieces[w], axis=0, keepdims=True)
-                highest = jnp.maximum(highest, jnp.where(valid[w], top, -1e30))
-            shift = highest * EXP2_SCALE
-            weights = [
-                jnp.exp2(
-                    piece * EXP2_SCALE
-                    - (shift if w == REACH - 1 else jnp.where(valid[w], shift, 1e30))
-                )
-                for w, piece in enumerate(pieces)
-            ]
-            weights = jnp.concatenate(weights, axis=0)
-            total = jnp.sum(weights, axis=0, keepdims=True)
-            probs = weights * (1.0 / total)
-            probs_low = probs.astype(jnp.bfloat16)
-            att_t = jnp.dot(
-                vt[:, low:high], probs_low, preferred_element_type=jnp.float32
+            qs[half, pl.ds(column, 2 * BLOCK), :] = q2
+            columns = pl.ds(column, 2 * BLOCK)
+            highest = None
+            for w in range(REACH):
+                at = low + w * BLOCK
+                score = jnp.dot(kw[at : at + BLOCK, :], qt, preferred_element_type=jnp.float32)
+                if w == REACH - 1:
+                    score = jnp.where(causal, score, -1e30)
+                scores[half, w * BLOCK : (w + 1) * BLOCK, :] = score
+                top = over_sublanes(jnp.max, score)
+                if w < REACH - 1:
+                    top = jnp.where(valid[w], top, -1e30)
+                highest = top if highest is None else jnp.maximum(highest, top)
+            shift = jnp.max(highest, axis=0, keepdims=True) * EXP2_SCALE
+            total = None
+            for w in range(REACH):
+                rows = pl.ds(w * BLOCK, BLOCK)
+                down = shift if w == REACH - 1 else jnp.where(valid[w], shift, 1e30)
+                weight = jnp.exp2(scores[half, rows, :] * EXP2_SCALE - down)
+                part = over_sublanes(jnp.sum, weight)
+                total = part if total is None else total + part
+                weights[half, rows, columns] = weight.astype(jnp.bfloat16)
+            inverse = 1.0 / jnp.sum(total, axis=0, keepdims=True)
+            att_t = (
+                jnp.dot(
+                    vt[:, low:high], weights[half, :, columns], preferred_element_type=jnp.float32
+                )
+                * inverse
             ).astype(jnp.bfloat16)
+            scaled_t = (gt.astype(jnp.float32) * inverse).astype(jnp.bfloat16)
+            gs[half, pl.ds(column, 2 * BLOCK), :] = scaled_t.T
             delta = jnp.sum(
-                gt.astype(jnp.float32) * att_t.astype(jnp.float32), axis=0, keepdims=True
+                scaled_t.astype(jnp.float32) * att_t.astype(jnp.float32), axis=0, keepdims=True
             )
-            grad_probs = jnp.dot(vw[low:high, :], gt, preferred_element_type=jnp.float32)
-            grad_scores = (probs * (grad_probs - delta)).astype(jnp.bfloat16)
+            for w in range(REACH):
+                at = low + w * BLOCK
+                rows = pl.ds(w * BLOCK, BLOCK)
+                grad = jnp.dot(
+                    vw[at : at + BLOCK, :], scaled_t, preferred_element_type=jnp.float32
+                )
+                grads[half, rows, columns] = (
+                    weights[half, rows, columns].astype(jnp.float32) * (grad - delta)
+                ).astype(jnp.bfloat16)
             gq_t = (
-                jnp.dot(kt[:, low:high], grad_scores, preferred_element_type=jnp.float32) * SCALE
+                jnp.dot(
+                    kt[:, low:high], grads[half, :, columns], preferred_element_type=jnp.float32
+                )
+                * SCALE
             ).astype(jnp.bfloat16)
-            dv[low:high, :] += jnp.dot(probs_low, g2, preferred_element_type=jnp.float32)
-            dk[low:high, :] += jnp.dot(grad_scores, q2, preferred_element_type=jnp.float32)
             rows = pl.ds(half * BLOCK, BLOCK)
             for i in range(2):
-                columns = pl.ds(pl.multiple_of(column + i * HD, HD), HD)
-                att_ref[rows, columns] = att_t[:, i * BLOCK : (i + 1) * BLOCK].T
-                gq_ref[rows, columns] = gq_t[:, i * BLOCK : (i + 1) * BLOCK].T
-        return 0
-
-    lax.fori_loop(0, HEADS // 2, pair_of_heads, 0)
+                out = pl.ds(column + i * HD, HD)
+                att_ref[rows, out] = att_t[:, i * BLOCK : (i + 1) * BLOCK].T
+                gq_ref[rows, out] = gq_t[:, i * BLOCK : (i + 1) * BLOCK].T
+
+    for pair in range(HEADS // 2):
+        pair_of_heads(pair)
+    for out, left, right in ((dv, weights, gs), (dk, grads, qs)):
+        for half in range(2):
+            added = jnp.dot(left[half], right[half], preferred_element_type=jnp.float32)
+            if half == 0:
+                out[0:1024, :] = added
+                out[1024:1152, :] = jnp.zeros((BLOCK, HD), jnp.float32)
+            else:
+                out[128:1152, :] += added
 
     for part, (total, factor) in enumerate(((dk, SCALE), (dv, None))):
         scaled = total[...] if factor is None else total[...] * factor
@@ -137,6 +160,11 @@
             pltpu.VMEM((HD, window), jnp.bfloat16),
             pltpu.VMEM((window, HD), jnp.float32),
             pltpu.VMEM((window, HD), jnp.float32),
+            pltpu.VMEM((2, REACH * BLOCK, 2 * BLOCK), jnp.float32),
+            pltpu.VMEM((2, REACH * BLOCK, HEADS * BLOCK), jnp.bfloat16),
+            pltpu.VMEM((2, REACH * BLOCK, HEADS * BLOCK), jnp.bfloat16),
+            pltpu.VMEM((2, HEADS * BLOCK, HD), jnp.bfloat16),
+            pltpu.VMEM((2, HEADS * BLOCK, HD), jnp.bfloat16),
         ],
         compiler_params=pltpu.CompilerParams(vmem_limit_bytes=40 * 1024 * 1024),
         cost_estimate=pl.CostEstimate(
@@ -155,33 +183,87 @@
     return lax.ppermute(block, "seq", [(i, i ^ 1) for i in range(lax.axis_size("seq"))])
 
 
-def by_group(array):
-    groups = lax.axis_size("head")
-    rows, columns = array.shape
-    return jnp.transpose(array.reshape(rows, groups, columns // groups), (1, 0, 2))
-
-
-def to_groups(chunks):
+def exchanged(chunks):
     received = lax.all_to_all(chunks, "head", split_axis=0, concat_axis=0, tiled=True)
     return received.reshape(-1, chunks.shape[2])
 
 
+def packing_kernel(queries_ref, grad_out_ref, keys_ref, values_ref, chunks_ref, kv_ref, sems):
+    groups, _, width = chunks_ref.shape
+    copies = []
+    for part, source in enumerate((queries_ref, grad_out_ref)):
+        half = width // 2
+        for group in range(groups):
+            copies.append(
+                pltpu.make_async_copy(
+                    source.at[:, pl.ds(group * half, half)],
+                    chunks_ref.at[group, :, pl.ds(part * half, half)],
+                    sems.at[part, group],
+                )
+            )
+    for part, source in enumerate((keys_ref, values_ref)):
+        columns = source.shape[1]
+        copies.append(
+            pltpu.make_async_copy(
+                source, kv_ref.at[:, pl.ds(part * columns, columns)], sems.at[2, part]
+            )
+        )
+    for copy in copies:
+        copy.start()
+    for copy in copies:
+        copy.wait()
+
+
+def packed(queries, keys, values, grad_out):
+    groups = lax.axis_size("head")
+    rows, columns = queries.shape
+    anywhere = pl.BlockSpec(memory_space=pl.ANY)
+    return pl.pallas_call(
+        packing_kernel,
+        out_shape=(
+            jax.ShapeDtypeStruct((groups, rows, 2 * columns // groups), queries.dtype),
+            jax.ShapeDtypeStruct((rows, 2 * keys.shape[1]), keys.dtype),
+        ),
+        in_specs=[anywhere] * 4,
+        out_specs=(anywhere, anywhere),
+        scratch_shapes=[pltpu.SemaphoreType.DMA((3, groups))],
+        cost_estimate=pl.CostEstimate(flops=0, bytes_accessed=2_400_000, transcendentals=0),
+        compiler_params=pltpu.CompilerParams(vmem_limit_bytes=8 * 1024 * 1024),
+    )(queries, grad_out, keys, values)
+
+
+def piling_kernel(own_ref, two_ref, four_ref, chunks_ref):
+    groups, _, width = chunks_ref.shape
+    half = own_ref.shape[1] // 2
+    for piece, source in enumerate((own_ref, two_ref, four_ref)):
+        for part in range(2):
+            for group in range(groups):
+                at = (2 * piece + part) * HD
+                chunks_ref[group, :, at : at + HD] = source[
+                    :, part * half + group * HD : part * half + (group + 1) * HD
+                ]
+
+
+def piled(own, two_back, four_back):
+    groups = lax.axis_size("head")
+    vmem = pl.BlockSpec(memory_space=pltpu.VMEM)
+    return pl.pallas_call(
+        piling_kernel,
+        out_shape=jax.ShapeDtypeStruct((groups, own.shape[0], 6 * HD), own.dtype),
+        in_specs=[vmem] * 3,
+        out_specs=vmem,
+        cost_estimate=pl.CostEstimate(flops=0, bytes_accessed=800_000, transcendentals=0),
+        compiler_params=pltpu.CompilerParams(vmem_limit_bytes=8 * 1024 * 1024),
+    )(own, two_back, four_back)
+
+
 def local(queries, keys, values, grad_out, doc_blocks):
-    keys_values = jnp.concatenate([keys, values], axis=1)
+    chunks, keys_values = packed(queries, keys, values, grad_out)
+    qg = exchanged(chunks)
     two_back = shifted(keys_values, 2)
     four_back = shifted(keys_values, 4)
-    qg = to_groups(jnp.concatenate([by_group(queries), by_group(grad_out)], axis=2))
-    width = keys.shape[1]
-    mine = to_groups(
-        jnp.concatenate(
-            [
-                by_group(array[:, at : at + width])
-                for array in (keys_values, two_back, four_back)
-                for at in (0, width)
-            ],
-            axis=2,
-        )
-    )
+    pile, qg = lax.optimization_barrier((piled(keys_values, two_back, four_back), qg))
+    mine = exchanged(pile)
     theirs = partners(mine)
     attended, grad_queries, kept, sent = attention(doc_blocks, qg, mine, theirs)
     odd = lax.rem(lax.axis_index("seq"), 2) == 1

time: 84 us -> 71.4 us (0.85)
  blocking collectives: 0 us -> 12.3 us
  waiting for transfers between devices: 29.2 us -> 17.8 us
  starting transfers between devices: 29.1 us -> 23.1 us
  local copies, waits for them, and re-layouts: 8.01 us -> 4.42 us
  Pallas kernels: 14.7 us -> 11.8 us
  other arithmetic: 1.27 us -> 0.2 us
    all_to_all x2 -> x1, waiting for transfers between devices: 16.1 us -> 0.01 us  [exchanged(): lax.all_to_all(chunks, 'head', split_axis=0, concat_axis=0, tiled=True)]
    all_to_all x0 -> x1, blocking collectives: none -> 12.3 us  [exchanged(): lax.all_to_all(chunks, 'head', split_axis=0, concat_axis=0, tiled=True)]
    ppermute x4, waiting for transfers between devices: 9.84 us -> 14.6 us  [shifted(): return lax.ppermute(block, 'seq', route)]
    all_to_all x2 -> x1, starting transfers between devices: 10.6 us -> 5.94 us  [exchanged(): lax.all_to_all(chunks, 'head', split_axis=0, concat_axis=0, tiled=True)]
    pallas_call x1, Pallas kernels: 14.7 us -> 10.5 us  [attention(): pl.pallas_call(attention_kernel, out_shape=(jax.ShapeDtypeStruct((ROWS, H...]
    unnamed x14 -> x10, local copies, waits for them, and re-layouts: 5.77 us -> 3.76 us
    concatenate x2 -> x0, local copies, waits for them, and re-layouts: 1.48 us -> none  [the longest x1 0.84 us: local(): keys_values = jnp.concatenate([keys, values], axis=1)]
    ppermute x4, starting transfers between devices: 18.5 us -> 17 us  [shifted(): return lax.ppermute(block, 'seq', route)]
  transfers between devices with their start and end apart: 8 -> 7, of which waited for: 7 -> 5; matrix products, arithmetic and copies ran while one was open for 7% -> 0% of each run, Pallas kernels for 0% -> 0%
where the time goes in v2:
time: 71.4 us; the launch traced here: 70.3 us
  starting transfers between devices  23.1 us (32%)
  waiting for transfers between devices  17.8 us (25%)
  blocking collectives  12.3 us (17%)
  Pallas kernels  11.8 us (17%)
  local copies, waits for them, and re-layouts  4.42 us (6%)
  between operations  0.72 us (1%)
    ppermute x4, starting transfers between devices, shifted(): return lax.ppermute(block, 'seq', route)  17 us
    ppermute x4, waiting for transfers between devices, shifted(): return lax.ppermute(block, 'seq', route)  14.6 us
    all_to_all x1, blocking collectives, exchanged(): lax.all_to_all(chunks, 'head', split_axis=0, concat_axis=0, tiled=True)  12.3 us
    pallas_call x1, Pallas kernels, attention(): pl.pallas_call(attention_kernel, out_shape=(jax.ShapeDtypeStruct((ROWS, H...  10.5 us
    all_to_all x1, starting transfers between devices, exchanged(): lax.all_to_all(chunks, 'head', split_axis=0, concat_axis=0, tiled=True)  5.94 us
    unnamed x10, local copies, waits for them, and re-layouts  3.76 us
    ppermute x2, waiting for transfers between devices, partners(): lax.ppermute(block, 'seq', [(i, i ^ 1) for i in range(lax.axis_size('seq'...  3.12 us
  transfers between devices with their start and end apart: 7, of which 5 were waited for; matrix products, arithmetic and copies ran while one was open for 0% of the time, Pallas kernels for 0%

profile of v2, /device:TPU:6, one launch (start us, length us, event | category | flops | bytes accessed | tf_op | source)
XLA Modules:
  0.0 70.3 jit_solution(5801414983836935959)
XLA Ops:
  0.6 0.0 copy-start
  0.6 1.0 %copy-done = bf16[32,8192]{1,0:T(8,128)(2,1)S(1)} copy-done((bf16[32,8192]{1,0:T(8,128)(2,1)S(1)}, bf16[32,8192]{1,0:T(8,128)(2,1)}, u32[]{:S(2)}) %copy-start) | copy-done | bytes 524312
  1.7 0.0 copy-start.1
  1.7 1.0 %copy-done.1 = bf16[32,8192]{1,0:T(8,128)(2,1)S(1)} copy-done((bf16[32,8192]{1,0:T(8,128)(2,1)S(1)}, bf16[32,8192]{1,0:T(8,128)(2,1)}, u32[]{:S(2)}) %copy-start.1) | copy-done | bytes 524312
  2.7 0.0 copy-start.2
  2.7 0.8 %copy-done.2 = bf16[32,1024]{1,0:T(8,128)(2,1)S(1)} copy-done((bf16[32,1024]{1,0:T(8,128)(2,1)S(1)}, bf16[32,1024]{1,0:T(8,128)(2,1)}, u32[]{:S(2)}) %copy-start.2) | copy-done | bytes 65560
  3.6 0.0 copy-start.3
  3.6 0.8 %copy-done.3 = bf16[32,1024]{1,0:T(8,128)(2,1)S(1)} copy-done((bf16[32,1024]{1,0:T(8,128)(2,1)S(1)}, bf16[32,1024]{1,0:T(8,128)(2,1)}, u32[]{:S(2)}) %copy-start.3) | copy-done | bytes 65560
  4.4 1.2 %shard_map.84 = (bf16[8,32,2048]{2,1,0:T(8,128)(2,1)}, bf16[32,2048]{1,0:T(8,128)(2,1)S(1)}) custom-call(bf16[32,8192]{1,0:T(8,128)(2,1)S(1)} %copy-done, bf16[32,8192]{1,0:T(8,128)(2,1)S(1)} %copy-done.1, bf16[32,1024]{1,0:T(8,128)(2,1)S(1)} %copy-done.2, bf16[32,1024]{1,0:T(8,128)(2,1)S(1)} %copy-done.3), custom_call_target="tpu_custom_call" | custom-call | bytes 2400000 | tf_op jit(solution)/shard_map/pallas_call | solution.py:221
  5.6 5.9 %all-to-all-start = ((bf16[8,32,2048]{2,1,0:T(8,128)(2,1)}), bf16[8,32,2048]{2,1,0:T(8,128)(2,1)S(1)}, u32[]{:S(2)}, u32[]{:S(2)}) async-start(bf16[8,32,2048]{2,1,0:T(8,128)(2,1)} %get-tuple-element.13), calls=%async_computation | async-start | bytes 2097152 | tf_op jit(solution)/shard_map/all_to_all | solution.py:187
  11.6 3.8 %collective-permute-start = (bf16[32,2048]{1,0:T(8,128)(2,1)S(1)}, bf16[32,2048]{1,0:T(8,128)(2,1)S(1)}, u32[]{:S(2)}, u32[]{:S(2)}) collective-permute-start(bf16[32,2048]{1,0:T(8,128)(2,1)S(1)} %get-tuple-element.12.own_ref), channel_id=1, source_target_pairs={{0,16},{8,24},{16,32},{24,40},{32,48},{40,56},{48,64},{56,72},{64,... | collective-permute-start | bytes 393224 | tf_op jit(solution)/shard_map/ppermute | solution.py:179
  15.4 5.2 %collective-permute-start.1 = (bf16[32,2048]{1,0:T(8,128)(2,1)S(1)}, bf16[32,2048]{1,0:T(8,128)(2,1)S(1)}, u32[]{:S(2)}, u32[]{:S(2)}) collective-permute-start(bf16[32,2048]{1,0:T(8,128)(2,1)S(1)} %get-tuple-element.12.own_ref), channel_id=1, source_target_pairs={{0,32},{8,40},{16,48},{24,56},{32,64},{40,72},{48,80},{56,88},{64,... | collective-permute-start | bytes 393224 | tf_op jit(solution)/shard_map/ppermute | solution.py:179
  20.6 2.6 %collective-permute-done.two_ref = bf16[32,2048]{1,0:T(8,128)(2,1)S(1)} collective-permute-done((bf16[32,2048]{1,0:T(8,128)(2,1)S(1)}, bf16[32,2048]{1,0:T(8,128)(2,1)S(1)}, u32[]{:S(2)}, u32[]{:S(2)}) %collective-permute-start) | collective-permute-done | bytes 131104 | tf_op jit(solution)/shard_map/ppermute | solution.py:179
  23.2 5.8 %collective-permute-done.1.four_ref = bf16[32,2048]{1,0:T(8,128)(2,1)S(1)} collective-permute-done((bf16[32,2048]{1,0:T(8,128)(2,1)S(1)}, bf16[32,2048]{1,0:T(8,128)(2,1)S(1)}, u32[]{:S(2)}, u32[]{:S(2)}) %collective-permute-start.1) | collective-permute-done | bytes 131104 | tf_op jit(solution)/shard_map/ppermute | solution.py:179
  29.0 0.1 shard_map.85
  29.1 0.0 all-to-all-done
  29.1 12.3 %all_to_all.10 = bf16[8,32,768]{2,1,0:T(8,128)(2,1)S(1)} all-to-all(bf16[8,32,768]{2,1,0:T(8,128)(2,1)S(1)} %shard_map.85), channel_id=1, replica_groups=mesh['seq'=32,'head'=8] {'head'}, dimensions={0} | all-to-all | bytes 786432 | tf_op jit(solution)/shard_map/all_to_all | solution.py:187
  41.4 0.0 copy-start.4
  41.4 0.0 collective-permute-start.2
  41.4 1.7 %collective-permute-done.2.theirs_ref = bf16[256,768]{1,0:T(8,128)(2,1)S(1)} collective-permute-done((bf16[256,768]{1,0:T(8,128)(2,1)S(1)}, bf16[256,768]{1,0:T(8,128)(2,1)S(1)}, u32[]{:S(2)}, u32[]{:S(2)}) %collective-permute-start.2) | collective-permute-done | bytes 393248 | tf_op jit(solution)/shard_map/ppermute | solution.py:183
  43.1 0.0 copy-done.4
  43.1 10.5 %shard_map.86 = (bf16[256,1024]{1,0:T(8,128)(2,1)}, bf16[256,1024]{1,0:T(8,128)(2,1)}, f32[256,768]{1,0:T(8,128)S(1)}, bf16[256,512]{1,0:T(8,128)(2,1)S(1)}) custom-call(s32[16]{0:T(128)S(1)} %copy-done.4, bf16[256,2048]{1,0:T(8,128)(2,1)S(1)} %bitcast.2, bf16[256,768]{1,0:T(8,128)(2,1)S(1)} %bitcast.4, bf16[256,768]{1,0:T(8,128)(2,1)S(1)} %collective-permute-done.2.theirs_ref), custom_call_target="tpu_custom_call" | custom-call | flops 3000000000 | bytes 4000000 | tf_op jit(solution)/shard_map/pallas_call | solution.py:146
  53.6 0.1 collective-permute-start.3
  53.7 1.4 %collective-permute-done.3 = bf16[256,512]{1,0:T(8,128)(2,1)S(1)} collective-permute-done((bf16[256,512]{1,0:T(8,128)(2,1)S(1)}, bf16[256,512]{1,0:T(8,128)(2,1)S(1)}, u32[]{:S(2)}, u32[]{:S(2)}) %collective-permute-start.3) | collective-permute-done | bytes 262176 | tf_op jit(solution)/shard_map/ppermute | solution.py:183
  55.2 0.1 add_convert_fusion.2
  55.3 4.7 %collective-permute-start.4 = (bf16[256,256]{1,0:T(8,128)(2,1)S(1)}, bf16[256,256]{1,0:T(8,128)(2,1)S(1)}, u32[]{:S(2)}, u32[]{:S(2)}) collective-permute-start(bf16[256,256]{1,0:T(8,128)(2,1)S(1)} %get-tuple-element.20), channel_id=1, source_target_pairs={{16,0},{24,8},{32,16},{40,24},{48,32},{56,40},{64,48},{72,56},{80,... | collective-permute-start | bytes 393224 | tf_op jit(solution)/shard_map/ppermute | solution.py:179
  60.0 3.4 %collective-permute-start.5 = (bf16[256,256]{1,0:T(8,128)(2,1)S(1)}, bf16[256,256]{1,0:T(8,128)(2,1)S(1)}, u32[]{:S(2)}, u32[]{:S(2)}) collective-permute-start(bf16[256,256]{1,0:T(8,128)(2,1)S(1)} %get-tuple-element.21), channel_id=1, source_target_pairs={{32,0},{40,8},{48,16},{56,24},{64,32},{72,40},{80,48},{88,56},{96,... | collective-permute-start | bytes 393224 | tf_op jit(solution)/shard_map/ppermute | solution.py:179
  63.3 0.0 collective-permute-done.4
  63.3 6.2 %collective-permute-done.5 = bf16[256,256]{1,0:T(8,128)(2,1)S(1)} collective-permute-done((bf16[256,256]{1,0:T(8,128)(2,1)S(1)}, bf16[256,256]{1,0:T(8,128)(2,1)S(1)}, u32[]{:S(2)}, u32[]{:S(2)}) %collective-permute-start.5) | collective-permute-done | bytes 131104 | tf_op jit(solution)/shard_map/ppermute | solution.py:179
  69.6 0.1 add_convert_fusion
  69.6 0.7 fusion
  (1 shorter events, 0.0 us)
Async XLA Ops:
  0.6 1.0 %copy-start = (bf16[32,8192]{1,0:T(8,128)(2,1)S(1)}, bf16[32,8192]{1,0:T(8,128)(2,1)}, u32[]{:S(2)}) copy-start(bf16[32,8192]{1,0:T(8,128)(2,1)} %queries_ref.1) | copy-start | bytes 1572868
  1.7 1.0 %copy-start.1 = (bf16[32,8192]{1,0:T(8,128)(2,1)S(1)}, bf16[32,8192]{1,0:T(8,128)(2,1)}, u32[]{:S(2)}) copy-start(bf16[32,8192]{1,0:T(8,128)(2,1)} %grad_out_ref.1) | copy-start | bytes 1572868
  2.7 0.8 %copy-start.2 = (bf16[32,1024]{1,0:T(8,128)(2,1)S(1)}, bf16[32,1024]{1,0:T(8,128)(2,1)}, u32[]{:S(2)}) copy-start(bf16[32,1024]{1,0:T(8,128)(2,1)} %keys_ref.1) | copy-start | bytes 196612
  3.6 0.8 %copy-start.3 = (bf16[32,1024]{1,0:T(8,128)(2,1)S(1)}, bf16[32,1024]{1,0:T(8,128)(2,1)}, u32[]{:S(2)}) copy-start(bf16[32,1024]{1,0:T(8,128)(2,1)} %values_ref.1) | copy-start | bytes 196612
  5.6 23.4 %all-to-all-start = ((bf16[8,32,2048]{2,1,0:T(8,128)(2,1)}), bf16[8,32,2048]{2,1,0:T(8,128)(2,1)S(1)}, u32[]{:S(2)}, u32[]{:S(2)}) async-start(bf16[8,32,2048]{2,1,0:T(8,128)(2,1)} %get-tuple-element.13), calls=%async_computation | async-start | bytes 2097152 | tf_op jit(solution)/shard_map/all_to_all | solution.py:187
  11.6 11.6 %collective-permute-start = (bf16[32,2048]{1,0:T(8,128)(2,1)S(1)}, bf16[32,2048]{1,0:T(8,128)(2,1)S(1)}, u32[]{:S(2)}, u32[]{:S(2)}) collective-permute-start(bf16[32,2048]{1,0:T(8,128)(2,1)S(1)} %get-tuple-element.12.own_ref), channel_id=1, source_target_pairs={{0,16},{8,24},{16,32},{24,40},{32,48},{40,56},{48,64},{56,72},{64,... | collective-permute-start | bytes 393224 | tf_op jit(solution)/shard_map/ppermute | solution.py:179
  15.4 13.6 %collective-permute-start.1 = (bf16[32,2048]{1,0:T(8,128)(2,1)S(1)}, bf16[32,2048]{1,0:T(8,128)(2,1)S(1)}, u32[]{:S(2)}, u32[]{:S(2)}) collective-permute-start(bf16[32,2048]{1,0:T(8,128)(2,1)S(1)} %get-tuple-element.12.own_ref), channel_id=1, source_target_pairs={{0,32},{8,40},{16,48},{24,56},{32,64},{40,72},{48,80},{56,88},{64,... | collective-permute-start | bytes 393224 | tf_op jit(solution)/shard_map/ppermute | solution.py:179
  41.4 1.7 %copy-start.4 = (s32[16]{0:T(128)S(1)}, s32[16]{0:T(128)}, u32[]{:S(2)}) copy-start(s32[16]{0:T(128)} %doc_ref.1) | copy-start | bytes 196
  41.4 1.7 %collective-permute-start.2 = (bf16[256,768]{1,0:T(8,128)(2,1)S(1)}, bf16[256,768]{1,0:T(8,128)(2,1)S(1)}, u32[]{:S(2)}, u32[]{:S(2)}) collective-permute-start(bf16[256,768]{1,0:T(8,128)(2,1)S(1)} %bitcast.3), channel_id=1, source_target_pairs={{0,8},{8,0},{16,24},{24,16},{32,40},{40,32},{48,56},{56,48},{64,72... | collective-permute-start | bytes 1179656 | tf_op jit(solution)/shard_map/ppermute | solution.py:183
  53.6 1.5 %collective-permute-start.3 = (bf16[256,512]{1,0:T(8,128)(2,1)S(1)}, bf16[256,512]{1,0:T(8,128)(2,1)S(1)}, u32[]{:S(2)}, u32[]{:S(2)}) collective-permute-start(bf16[256,512]{1,0:T(8,128)(2,1)S(1)} %get-tuple-element.19), channel_id=1, source_target_pairs={{0,8},{8,0},{16,24},{24,16},{32,40},{40,32},{48,56},{56,48},{64,72... | collective-permute-start | bytes 786440 | tf_op jit(solution)/shard_map/ppermute | solution.py:183
  55.3 8.1 %collective-permute-start.4 = (bf16[256,256]{1,0:T(8,128)(2,1)S(1)}, bf16[256,256]{1,0:T(8,128)(2,1)S(1)}, u32[]{:S(2)}, u32[]{:S(2)}) collective-permute-start(bf16[256,256]{1,0:T(8,128)(2,1)S(1)} %get-tuple-element.20), channel_id=1, source_target_pairs={{16,0},{24,8},{32,16},{40,24},{48,32},{56,40},{64,48},{72,56},{80,... | collective-permute-start | bytes 393224 | tf_op jit(solution)/shard_map/ppermute | solution.py:179
  60.0 9.6 %collective-permute-start.5 = (bf16[256,256]{1,0:T(8,128)(2,1)S(1)}, bf16[256,256]{1,0:T(8,128)(2,1)S(1)}, u32[]{:S(2)}, u32[]{:S(2)}) collective-permute-start(bf16[256,256]{1,0:T(8,128)(2,1)S(1)} %get-tuple-element.21), channel_id=1, source_target_pairs={{32,0},{40,8},{48,16},{56,24},{64,32},{72,40},{80,48},{88,56},{96,... | collective-permute-start | bytes 393224 | tf_op jit(solution)/shard_map/ppermute | solution.py:179

commit v3 on v2

--- a/solution.py
+++ b/solution.py
@@ -25,22 +25,35 @@
 
 
 def attention_kernel(
-    doc_ref, qg_ref, mine_ref, theirs_ref,
+    doc_ref, qg_ref, own_ref, two_ref, four_ref, their_two_ref, their_other_ref,
     att_ref, gq_ref, kept_ref, sent_ref,
     kw, vw, kt, vt, dk, dv, scores, weights, grads, qs, gs,
 ):
     here = lax.axis_index("seq")
     parity = lax.rem(here, 2)
-    far = pl.multiple_of(512 - 256 * parity, 128)
-    near = pl.multiple_of(256 - 256 * parity, 128)
-    for part, (window, turned) in enumerate(((kw, kt), (vw, vt))):
-        at = part * HD
-        window[0:128, :] = mine_ref[128:256, 512 + at : 512 + at + HD]
-        window[128:384, :] = theirs_ref[:, pl.ds(far + at, HD)]
-        window[384:640, :] = mine_ref[:, 256 + at : 256 + at + HD]
-        window[640:896, :] = theirs_ref[:, pl.ds(near + at, HD)]
-        window[896:1152, :] = mine_ref[:, at : at + HD]
-        turned[...] = window[...].T
+    for part, window in enumerate((kw, vw)):
+        columns = pl.ds(part * HD, HD)
+        window[0:128, :] = four_ref[128:256, columns]
+        window[384:640, :] = two_ref[:, columns]
+        window[896:1152, :] = own_ref[:, columns]
+
+    @pl.when(parity == 0)
+    def _():
+        for part, window in enumerate((kw, vw)):
+            columns = pl.ds(part * HD, HD)
+            window[128:384, :] = their_other_ref[:, columns]
+            window[640:896, :] = their_two_ref[:, columns]
+
+    @pl.when(parity == 1)
+    def _():
+        for part, window in enumerate((kw, vw)):
+            columns = pl.ds(part * HD, HD)
+            window[128:384, :] = their_two_ref[:, columns]
+            window[640:896, :] = their_other_ref[:, columns]
+
+    kt[...] = kw[...].T
+    vt[...] = vw[...].T
+
     starts = [document_start(doc_ref, 2 * here + half) for half in range(2)]
     key_at = lax.broadcasted_iota(jnp.int32, (BLOCK, 2 * BLOCK), 0)
     query_at = lax.rem(lax.broadcasted_iota(jnp.int32, (BLOCK, 2 * BLOCK), 1), BLOCK)
@@ -140,7 +153,7 @@
         sent_ref[:, 256 + at : 256 + at + HD] = scaled[128:384, :].astype(jnp.bfloat16)
 
 
-def attention(doc_blocks, qg, mine, theirs):
+def attention(doc_blocks, qg, *pieces):
     vmem = pl.BlockSpec(memory_space=pltpu.VMEM)
     window = WINDOW * BLOCK
     return pl.pallas_call(
@@ -151,7 +164,7 @@
             jax.ShapeDtypeStruct((ROWS, 6 * HD), jnp.float32),
             jax.ShapeDtypeStruct((ROWS, 4 * HD), jnp.bfloat16),
         ),
-        in_specs=[pl.BlockSpec(memory_space=pltpu.SMEM), vmem, vmem, vmem],
+        in_specs=[pl.BlockSpec(memory_space=pltpu.SMEM)] + [vmem] * 6,
         out_specs=(vmem, vmem, vmem, vmem),
         scratch_shapes=[
             pltpu.VMEM((window, HD), jnp.bfloat16),
@@ -170,7 +183,7 @@
         cost_estimate=pl.CostEstimate(
             flops=3_000_000_000, bytes_accessed=4_000_000, transcendentals=2_100_000
         ),
-    )(doc_blocks, qg, mine, theirs)
+    )(doc_blocks, qg, *pieces)
 
 
 def shifted(block, distance):
@@ -188,85 +201,70 @@
     return received.reshape(-1, chunks.shape[2])
 
 
-def packing_kernel(queries_ref, grad_out_ref, keys_ref, values_ref, chunks_ref, kv_ref, sems):
+def packing_kernel(queries_ref, grad_out_ref, chunks_ref, sems):
     groups, _, width = chunks_ref.shape
-    copies = []
-    for part, source in enumerate((queries_ref, grad_out_ref)):
-        half = width // 2
-        for group in range(groups):
-            copies.append(
-                pltpu.make_async_copy(
-                    source.at[:, pl.ds(group * half, half)],
-                    chunks_ref.at[group, :, pl.ds(part * half, half)],
-                    sems.at[part, group],
-                )
-            )
-    for part, source in enumerate((keys_ref, values_ref)):
-        columns = source.shape[1]
-        copies.append(
-            pltpu.make_async_copy(
-                source, kv_ref.at[:, pl.ds(part * columns, columns)], sems.at[2, part]
-            )
+    half = width // 2
+    copies = [
+        pltpu.make_async_copy(
+            source.at[:, pl.ds(group * half, half)],
+            chunks_ref.at[group, :, pl.ds(part * half, half)],
+            sems.at[part, group],
         )
+        for part, source in enumerate((queries_ref, grad_out_ref))
+        for group in range(groups)
+    ]
     for copy in copies:
         copy.start()
     for copy in copies:
         copy.wait()
 
 
-def packed(queries, keys, values, grad_out):
+def packed(queries, grad_out):
     groups = lax.axis_size("head")
     rows, columns = queries.shape
     anywhere = pl.BlockSpec(memory_space=pl.ANY)
     return pl.pallas_call(
         packing_kernel,
-        out_shape=(
-            jax.ShapeDtypeStruct((groups, rows, 2 * columns // groups), queries.dtype),
-            jax.ShapeDtypeStruct((rows, 2 * keys.shape[1]), keys.dtype),
-        ),
-        in_specs=[anywhere] * 4,
-        out_specs=(anywhere, anywhere),
-        scratch_shapes=[pltpu.SemaphoreType.DMA((3, groups))],
-        cost_estimate=pl.CostEstimate(flops=0, bytes_accessed=2_400_000, transcendentals=0),
-        compiler_params=pltpu.CompilerParams(vmem_limit_bytes=8 * 1024 * 1024),
-    )(queries, grad_out, keys, values)
-
-
-def piling_kernel(own_ref, two_ref, four_ref, chunks_ref):
-    groups, _, width = chunks_ref.shape
-    half = own_ref.shape[1] // 2
-    for piece, source in enumerate((own_ref, two_ref, four_ref)):
-        for part in range(2):
-            for group in range(groups):
-                at = (2 * piece + part) * HD
-                chunks_ref[group, :, at : at + HD] = source[
-                    :, part * half + group * HD : part * half + (group + 1) * HD
-                ]
-
-
-def piled(own, two_back, four_back):
+        out_shape=jax.ShapeDtypeStruct((groups, rows, 2 * columns // groups), queries.dtype),
+        in_specs=[anywhere] * 2,
+        out_specs=anywhere,
+        scratch_shapes=[pltpu.SemaphoreType.DMA((2, groups))],
+        cost_estimate=pl.CostEstimate(flops=0, bytes_accessed=2_100_000, transcendentals=0),
+    )(queries, grad_out)
+
+
+def piling_kernel(keys_ref, values_ref, chunks_ref):
+    for group in range(chunks_ref.shape[0]):
+        for part, source in enumerate((keys_ref, values_ref)):
+            chunks_ref[group, :, part * HD : (part + 1) * HD] = source[
+                :, group * HD : (group + 1) * HD
+            ]
+
+
+def piled(keys, values):
     groups = lax.axis_size("head")
     vmem = pl.BlockSpec(memory_space=pltpu.VMEM)
     return pl.pallas_call(
         piling_kernel,
-        out_shape=jax.ShapeDtypeStruct((groups, own.shape[0], 6 * HD), own.dtype),
-        in_specs=[vmem] * 3,
+        out_shape=jax.ShapeDtypeStruct((groups, keys.shape[0], 2 * HD), keys.dtype),
+        in_specs=[vmem] * 2,
         out_specs=vmem,
-        cost_estimate=pl.CostEstimate(flops=0, bytes_accessed=800_000, transcendentals=0),
-        compiler_params=pltpu.CompilerParams(vmem_limit_bytes=8 * 1024 * 1024),
-    )(own, two_back, four_back)
+        cost_estimate=pl.CostEstimate(flops=0, bytes_accessed=260_000, transcendentals=0),
+    )(keys, values)
 
 
 def local(queries, keys, values, grad_out, doc_blocks):
-    chunks, keys_values = packed(queries, keys, values, grad_out)
+    odd = lax.rem(lax.axis_index("seq"), 2) == 1
+    own = exchanged(piled(keys, values))
+    chunks, own = lax.optimization_barrier((packed(queries, grad_out), own))
     qg = exchanged(chunks)
-    two_back = shifted(keys_values, 2)
-    four_back = shifted(keys_values, 4)
-    pile, qg = lax.optimization_barrier((piled(keys_values, two_back, four_back), qg))
-    mine = exchanged(pile)
-    theirs = partners(mine)
-    attended, grad_queries, kept, sent = attention(doc_blocks, qg, mine, theirs)
-    odd = lax.rem(lax.axis_index("seq"), 2) == 1
+    two = shifted(own, 2)
+    four = shifted(own, 4)
+    their_two = partners(two)
+    their_other = partners(jnp.where(odd, four, own))
+    attended, grad_queries, kept, sent = attention(
+        doc_blocks, qg, own, two, four, their_two, their_other
+    )
     swapped = partners(sent).astype(jnp.float32)
     one, three = swapped[:, 0:256], swapped[:, 256:512]
     for_here = kept[:, 0:256] + jnp.where(odd, 0.0, one)

time: 71.4 us -> 93.2 us (1.31)
  Pallas kernels: 11.8 us -> 45.1 us
  blocking collectives: 12.3 us -> 0 us
  starting transfers between devices: 23.1 us -> 28.9 us
  local copies, waits for them, and re-layouts: 4.42 us -> 0.67 us
  waiting for transfers between devices: 17.8 us -> 16.8 us
    pallas_call x2, Pallas kernels: 1.28 us -> 34.6 us  [the longest x1 33 us: packed(): pl.pallas_call(packing_kernel, out_shape=jax.ShapeDtypeStruct((groups, ro...]
    all_to_all x1 -> x0, blocking collectives: 12.3 us -> none  [exchanged(): lax.all_to_all(chunks, 'head', split_axis=0, concat_axis=0, tiled=True)]
    all_to_all x1 -> x2, starting transfers between devices: 5.94 us -> 11.6 us  [exchanged(): lax.all_to_all(chunks, 'head', split_axis=0, concat_axis=0, tiled=True)]
    unnamed x10 -> x2, local copies, waits for them, and re-layouts: 3.76 us -> 0.01 us
    ppermute x2 -> x3, waiting for transfers between devices: 3.12 us -> 2.73 us  [partners(): lax.ppermute(block, 'seq', [(i, i ^ 1) for i in range(lax.axis_size('seq'...]
  transfers between devices with their start and end apart: 7 -> 9, of which waited for: 5 -> 5; matrix products, arithmetic and copies ran while one was open for 0% -> 0% of each run, Pallas kernels for 0% -> 36%
where the time goes in v3:
time: 93.2 us; the launch traced here: 92.4 us
  Pallas kernels  45.1 us (48%)
  starting transfers between devices  28.9 us (31%)
  waiting for transfers between devices  16.8 us (18%)
    pallas_call x1, Pallas kernels, packed(): pl.pallas_call(packing_kernel, out_shape=jax.ShapeDtypeStruct((groups, ro...  33 us
    ppermute x4, starting transfers between devices, shifted(): return lax.ppermute(block, 'seq', route)  17 us
    ppermute x4, waiting for transfers between devices, shifted(): return lax.ppermute(block, 'seq', route)  14.1 us
    all_to_all x2, starting transfers between devices, exchanged(): lax.all_to_all(chunks, 'head', split_axis=0, concat_axis=0, tiled=True)  11.6 us
    pallas_call x1, Pallas kernels, attention(): pl.pallas_call(attention_kernel, out_shape=(jax.ShapeDtypeStruct((ROWS, H...  10.6 us
    ppermute x3, waiting for transfers between devices, partners(): lax.ppermute(block, 'seq', [(i, i ^ 1) for i in range(lax.axis_size('seq'...  2.73 us
  transfers between devices with their start and end apart: 9, of which 5 were waited for; matrix products, arithmetic and copies ran while one was open for 0% of the time, Pallas kernels for 36%

profile of v3, /device:TPU:6, one launch (start us, length us, event | category | flops | bytes accessed | tf_op | source)
XLA Modules:
  0.0 92.4 jit_solution(9727765632856427248)
XLA Ops:
  0.6 1.6 %shard_map.85 = bf16[8,32,256]{2,1,0:T(8,128)(2,1)} custom-call(bf16[32,1024]{1,0:T(8,128)(2,1)} %keys_ref.1, bf16[32,1024]{1,0:T(8,128)(2,1)} %values_ref.1), custom_call_target="tpu_custom_call" | custom-call | bytes 260000 | tf_op jit(solution)/shard_map/pallas_call | solution.py:247
  2.2 5.9 %all-to-all-start = ((bf16[8,32,256]{2,1,0:T(8,128)(2,1)}), bf16[8,32,256]{2,1,0:T(8,128)(2,1)S(1)}, u32[]{:S(2)}, u32[]{:S(2)}) async-start(bf16[8,32,256]{2,1,0:T(8,128)(2,1)} %shard_map.85), calls=%async_computation | async-start | bytes 262144 | tf_op jit(solution)/shard_map/all_to_all | solution.py:200
  8.1 33.0 %shard_map.84 = bf16[8,32,2048]{2,1,0:T(8,128)(2,1)} custom-call(bf16[32,8192]{1,0:T(8,128)(2,1)} %queries_ref.1, bf16[32,8192]{1,0:T(8,128)(2,1)} %grad_out_ref.1), custom_call_target="tpu_custom_call" | custom-call | bytes 2100000 | tf_op jit(solution)/shard_map/pallas_call | solution.py:226
  41.1 0.0 all-to-all-done
  41.1 5.7 %all-to-all-start.1 = ((bf16[8,32,2048]{2,1,0:T(8,128)(2,1)}), bf16[8,32,2048]{2,1,0:T(8,128)(2,1)S(1)}, u32[]{:S(2)}, u32[]{:S(2)}) async-start(bf16[8,32,2048]{2,1,0:T(8,128)(2,1)} %shard_map.84), calls=%async_computation.1 | async-start | bytes 2097152 | tf_op jit(solution)/shard_map/all_to_all | solution.py:200
  46.8 5.2 %collective-permute-start.1 = (bf16[256,256]{1,0:T(8,128)(2,1)S(1)}, bf16[256,256]{1,0:T(8,128)(2,1)S(1)}, u32[]{:S(2)}, u32[]{:S(2)}) collective-permute-start(bf16[256,256]{1,0:T(8,128)(2,1)S(1)} %bitcast.3), channel_id=1, source_target_pairs={{0,32},{8,40},{16,48},{24,56},{32,64},{40,72},{48,80},{56,88},{64,... | collective-permute-start | bytes 393224 | tf_op jit(solution)/shard_map/ppermute | solution.py:192
  52.0 3.8 %collective-permute-start = (bf16[256,256]{1,0:T(8,128)(2,1)S(1)}, bf16[256,256]{1,0:T(8,128)(2,1)S(1)}, u32[]{:S(2)}, u32[]{:S(2)}) collective-permute-start(bf16[256,256]{1,0:T(8,128)(2,1)S(1)} %bitcast.4), channel_id=1, source_target_pairs={{0,16},{8,24},{16,32},{24,40},{32,48},{40,56},{48,64},{56,72},{64,... | collective-permute-start | bytes 393224 | tf_op jit(solution)/shard_map/ppermute | solution.py:192
  55.9 5.8 %collective-permute-done.1.four_ref = bf16[256,256]{1,0:T(8,128)(2,1)S(1)} collective-permute-done((bf16[256,256]{1,0:T(8,128)(2,1)S(1)}, bf16[256,256]{1,0:T(8,128)(2,1)S(1)}, u32[]{:S(2)}, u32[]{:S(2)}) %collective-permute-start.1) | collective-permute-done | bytes 131104 | tf_op jit(solution)/shard_map/ppermute | solution.py:192
  61.7 0.0 copy-start
  61.7 0.1 collective-permute-start.3
  61.8 1.6 %collective-permute-done.two_ref = bf16[256,256]{1,0:T(8,128)(2,1)S(1)} collective-permute-done((bf16[256,256]{1,0:T(8,128)(2,1)S(1)}, bf16[256,256]{1,0:T(8,128)(2,1)S(1)}, u32[]{:S(2)}, u32[]{:S(2)}) %collective-permute-start) | collective-permute-done | bytes 131104 | tf_op jit(solution)/shard_map/ppermute | solution.py:192
  63.4 0.0 collective-permute-start.2
  63.4 0.0 collective-permute-done.3.their_other_ref
  63.4 1.3 %collective-permute-done.2.their_two_ref = bf16[256,256]{1,0:T(8,128)(2,1)S(1)} collective-permute-done((bf16[256,256]{1,0:T(8,128)(2,1)S(1)}, bf16[256,256]{1,0:T(8,128)(2,1)S(1)}, u32[]{:S(2)}, u32[]{:S(2)}) %collective-permute-start.2) | collective-permute-done | bytes 131104 | tf_op jit(solution)/shard_map/ppermute | solution.py:196
  64.8 0.0 all-to-all-done.1
  64.8 0.0 copy-done
  64.8 10.6 %shard_map.86 = (bf16[256,1024]{1,0:T(8,128)(2,1)}, bf16[256,1024]{1,0:T(8,128)(2,1)}, f32[256,768]{1,0:T(8,128)S(1)}, bf16[256,512]{1,0:T(8,128)(2,1)S(1)}) custom-call(s32[16]{0:T(128)S(1)} %copy-done, bf16[256,2048]{1,0:T(8,128)(2,1)S(1)} %bitcast.2, bf16[256,256]{1,0:T(8,128)(2,1)S(1)} %bitcast.6, bf16[256,256]{1,0:T(8,128)(2,1)S(1)} %collective-permute-done.two_ref, ...), custom_call_target="tpu_custom_call" | custom-call | flops 3000000000 | bytes 4000000 | tf_op jit(solution)/shard_map/pallas_call | solution.py:159
  75.4 0.1 collective-permute-start.4
  75.5 1.4 %collective-permute-done.4 = bf16[256,512]{1,0:T(8,128)(2,1)S(1)} collective-permute-done((bf16[256,512]{1,0:T(8,128)(2,1)S(1)}, bf16[256,512]{1,0:T(8,128)(2,1)S(1)}, u32[]{:S(2)}, u32[]{:S(2)}) %collective-permute-start.4) | collective-permute-done | bytes 262176 | tf_op jit(solution)/shard_map/ppermute | solution.py:196
  76.9 0.1 convert_element_type.18
  77.0 0.1 add_convert_fusion.2
  77.0 4.6 %collective-permute-start.5 = (bf16[256,256]{1,0:T(8,128)(2,1)S(1)}, bf16[256,256]{1,0:T(8,128)(2,1)S(1)}, u32[]{:S(2)}, u32[]{:S(2)}) collective-permute-start(bf16[256,256]{1,0:T(8,128)(2,1)S(1)} %get-tuple-element.16), channel_id=1, source_target_pairs={{16,0},{24,8},{32,16},{40,24},{48,32},{56,40},{64,48},{72,56},{80,... | collective-permute-start | bytes 393224 | tf_op jit(solution)/shard_map/ppermute | solution.py:192
  81.7 3.3 %collective-permute-start.6 = (bf16[256,256]{1,0:T(8,128)(2,1)S(1)}, bf16[256,256]{1,0:T(8,128)(2,1)S(1)}, u32[]{:S(2)}, u32[]{:S(2)}) collective-permute-start(bf16[256,256]{1,0:T(8,128)(2,1)S(1)} %get-tuple-element.17), channel_id=1, source_target_pairs={{32,0},{40,8},{48,16},{56,24},{64,32},{72,40},{80,48},{88,56},{96,... | collective-permute-start | bytes 393224 | tf_op jit(solution)/shard_map/ppermute | solution.py:192
  85.0 0.0 collective-permute-done.5
  85.1 6.6 %collective-permute-done.6 = bf16[256,256]{1,0:T(8,128)(2,1)S(1)} collective-permute-done((bf16[256,256]{1,0:T(8,128)(2,1)S(1)}, bf16[256,256]{1,0:T(8,128)(2,1)S(1)}, u32[]{:S(2)}, u32[]{:S(2)}) %collective-permute-start.6) | collective-permute-done | bytes 131104 | tf_op jit(solution)/shard_map/ppermute | solution.py:192
  91.7 0.1 add_convert_fusion
  91.7 0.7 fusion
  (1 shorter events, 0.0 us)
Async XLA Ops:
  2.2 38.9 %all-to-all-start = ((bf16[8,32,256]{2,1,0:T(8,128)(2,1)}), bf16[8,32,256]{2,1,0:T(8,128)(2,1)S(1)}, u32[]{:S(2)}, u32[]{:S(2)}) async-start(bf16[8,32,256]{2,1,0:T(8,128)(2,1)} %shard_map.85), calls=%async_computation | async-start | bytes 262144 | tf_op jit(solution)/shard_map/all_to_all | solution.py:200
  41.1 23.7 %all-to-all-start.1 = ((bf16[8,32,2048]{2,1,0:T(8,128)(2,1)}), bf16[8,32,2048]{2,1,0:T(8,128)(2,1)S(1)}, u32[]{:S(2)}, u32[]{:S(2)}) async-start(bf16[8,32,2048]{2,1,0:T(8,128)(2,1)} %shard_map.84), calls=%async_computation.1 | async-start | bytes 2097152 | tf_op jit(solution)/shard_map/all_to_all | solution.py:200
  46.8 14.8 %collective-permute-start.1 = (bf16[256,256]{1,0:T(8,128)(2,1)S(1)}, bf16[256,256]{1,0:T(8,128)(2,1)S(1)}, u32[]{:S(2)}, u32[]{:S(2)}) collective-permute-start(bf16[256,256]{1,0:T(8,128)(2,1)S(1)} %bitcast.3), channel_id=1, source_target_pairs={{0,32},{8,40},{16,48},{24,56},{32,64},{40,72},{48,80},{56,88},{64,... | collective-permute-start | bytes 393224 | tf_op jit(solution)/shard_map/ppermute | solution.py:192
  52.0 11.4 %collective-permute-start = (bf16[256,256]{1,0:T(8,128)(2,1)S(1)}, bf16[256,256]{1,0:T(8,128)(2,1)S(1)}, u32[]{:S(2)}, u32[]{:S(2)}) collective-permute-start(bf16[256,256]{1,0:T(8,128)(2,1)S(1)} %bitcast.4), channel_id=1, source_target_pairs={{0,16},{8,24},{16,32},{24,40},{32,48},{40,56},{48,64},{56,72},{64,... | collective-permute-start | bytes 393224 | tf_op jit(solution)/shard_map/ppermute | solution.py:192
  61.7 3.1 %copy-start = (s32[16]{0:T(128)S(1)}, s32[16]{0:T(128)}, u32[]{:S(2)}) copy-start(s32[16]{0:T(128)} %doc_ref.1) | copy-start | bytes 196
  61.7 1.8 %collective-permute-start.3 = (bf16[256,256]{1,0:T(8,128)(2,1)S(1)}, bf16[256,256]{1,0:T(8,128)(2,1)S(1)}, u32[]{:S(2)}, u32[]{:S(2)}) collective-permute-start(bf16[256,256]{1,0:T(8,128)(2,1)S(1)} %broadcast_select_fusion), channel_id=1, source_target_pairs={{0,8},{8,0},{16,24},{24,16},{32,40},{40,32},{48,56},{56,48},{64,72... | collective-permute-start | bytes 393224 | tf_op jit(solution)/shard_map/ppermute | solution.py:196
  63.4 1.3 %collective-permute-start.2 = (bf16[256,256]{1,0:T(8,128)(2,1)S(1)}, bf16[256,256]{1,0:T(8,128)(2,1)S(1)}, u32[]{:S(2)}, u32[]{:S(2)}) collective-permute-start(bf16[256,256]{1,0:T(8,128)(2,1)S(1)} %collective-permute-done.two_ref), channel_id=1, source_target_pairs={{0,8},{8,0},{16,24},{24,16},{32,40},{40,32},{48,56},{56,48},{64,72... | collective-permute-start | bytes 393224 | tf_op jit(solution)/shard_map/ppermute | solution.py:196
  75.4 1.5 %collective-permute-start.4 = (bf16[256,512]{1,0:T(8,128)(2,1)S(1)}, bf16[256,512]{1,0:T(8,128)(2,1)S(1)}, u32[]{:S(2)}, u32[]{:S(2)}) collective-permute-start(bf16[256,512]{1,0:T(8,128)(2,1)S(1)} %get-tuple-element.15), channel_id=1, source_target_pairs={{0,8},{8,0},{16,24},{24,16},{32,40},{40,32},{48,56},{56,48},{64,72... | collective-permute-start | bytes 786440 | tf_op jit(solution)/shard_map/ppermute | solution.py:196
  77.0 8.0 %collective-permute-start.5 = (bf16[256,256]{1,0:T(8,128)(2,1)S(1)}, bf16[256,256]{1,0:T(8,128)(2,1)S(1)}, u32[]{:S(2)}, u32[]{:S(2)}) collective-permute-start(bf16[256,256]{1,0:T(8,128)(2,1)S(1)} %get-tuple-element.16), channel_id=1, source_target_pairs={{16,0},{24,8},{32,16},{40,24},{48,32},{56,40},{64,48},{72,56},{80,... | collective-permute-start | bytes 393224 | tf_op jit(solution)/shard_map/ppermute | solution.py:192
  81.7 10.0 %collective-permute-start.6 = (bf16[256,256]{1,0:T(8,128)(2,1)S(1)}, bf16[256,256]{1,0:T(8,128)(2,1)S(1)}, u32[]{:S(2)}, u32[]{:S(2)}) collective-permute-start(bf16[256,256]{1,0:T(8,128)(2,1)S(1)} %get-tuple-element.17), channel_id=1, source_target_pairs={{32,0},{40,8},{48,16},{56,24},{64,32},{72,40},{80,48},{88,56},{96,... | collective-permute-start | bytes 393224 | tf_op jit(solution)/shard_map/ppermute | solution.py:192

commit v4 on v3

--- a/solution.py
+++ b/solution.py
@@ -201,34 +201,47 @@
     return received.reshape(-1, chunks.shape[2])
 
 
-def packing_kernel(queries_ref, grad_out_ref, chunks_ref, sems):
+def packing_kernel(queries_ref, grad_out_ref, chunks_ref, held, in_sems, out_sems):
     groups, _, width = chunks_ref.shape
     half = width // 2
-    copies = [
-        pltpu.make_async_copy(
+
+    def arriving(part, group):
+        source = (queries_ref, grad_out_ref)[part]
+        return pltpu.make_async_copy(
             source.at[:, pl.ds(group * half, half)],
-            chunks_ref.at[group, :, pl.ds(part * half, half)],
-            sems.at[part, group],
+            held.at[group, :, pl.ds(part * half, half)],
+            in_sems.at[part, group],
         )
-        for part, source in enumerate((queries_ref, grad_out_ref))
-        for group in range(groups)
-    ]
-    for copy in copies:
-        copy.start()
-    for copy in copies:
-        copy.wait()
+
+    def leaving(group):
+        return pltpu.make_async_copy(held.at[group], chunks_ref.at[group], out_sems.at[group])
+
+    for group in range(groups):
+        for part in range(2):
+            arriving(part, group).start()
+    for group in range(groups):
+        for part in range(2):
+            arriving(part, group).wait()
+        leaving(group).start()
+    for group in range(groups):
+        leaving(group).wait()
 
 
 def packed(queries, grad_out):
     groups = lax.axis_size("head")
     rows, columns = queries.shape
+    chunks = (groups, rows, 2 * columns // groups)
     anywhere = pl.BlockSpec(memory_space=pl.ANY)
     return pl.pallas_call(
         packing_kernel,
-        out_shape=jax.ShapeDtypeStruct((groups, rows, 2 * columns // groups), queries.dtype),
+        out_shape=jax.ShapeDtypeStruct(chunks, queries.dtype),
         in_specs=[anywhere] * 2,
         out_specs=anywhere,
-        scratch_shapes=[pltpu.SemaphoreType.DMA((2, groups))],
+        scratch_shapes=[
+            pltpu.VMEM(chunks, queries.dtype),
+            pltpu.SemaphoreType.DMA((2, groups)),
+            pltpu.SemaphoreType.DMA((groups,)),
+        ],
         cost_estimate=pl.CostEstimate(flops=0, bytes_accessed=2_100_000, transcendentals=0),
     )(queries, grad_out)
 

time: 93.2 us -> 64.2 us (0.69)
  Pallas kernels: 45.1 us -> 14.2 us
  waiting for transfers between devices: 16.8 us -> 19.4 us
    pallas_call x1, Pallas kernels: 33 us -> 2.13 us  [packed(): pl.pallas_call(packing_kernel, out_shape=jax.ShapeDtypeStruct(chunks, que...]
    all_to_all x2, waiting for transfers between devices: 0.01 us -> 3.28 us  [exchanged(): lax.all_to_all(chunks, 'head', split_axis=0, concat_axis=0, tiled=True)]
    all_to_all x2, starting transfers between devices: 11.6 us -> 10.7 us  [exchanged(): lax.all_to_all(chunks, 'head', split_axis=0, concat_axis=0, tiled=True)]
  transfers between devices with their start and end apart: 9 -> 9, of which waited for: 5 -> 7; matrix products, arithmetic and copies ran while one was open for 0% -> 0% of each run, Pallas kernels for 36% -> 3%
where the time goes in v4:
time: 64.2 us; the launch traced here: 63.3 us
  starting transfers between devices  28.1 us (44%)
  waiting for transfers between devices  19.4 us (30%)
  Pallas kernels  14.2 us (22%)
  between operations  0.73 us (1%)
  local copies, waits for them, and re-layouts  0.67 us (1%)
    ppermute x4, starting transfers between devices, shifted(): return lax.ppermute(block, 'seq', route)  17.1 us
    ppermute x4, waiting for transfers between devices, shifted(): return lax.ppermute(block, 'seq', route)  13.4 us
    all_to_all x2, starting transfers between devices, exchanged(): lax.all_to_all(chunks, 'head', split_axis=0, concat_axis=0, tiled=True)  10.7 us
    pallas_call x1, Pallas kernels, attention(): pl.pallas_call(attention_kernel, out_shape=(jax.ShapeDtypeStruct((ROWS, H...  10.6 us
    all_to_all x2, waiting for transfers between devices, exchanged(): lax.all_to_all(chunks, 'head', split_axis=0, concat_axis=0, tiled=True)  3.28 us
    ppermute x3, waiting for transfers between devices, partners(): lax.ppermute(block, 'seq', [(i, i ^ 1) for i in range(lax.axis_size('seq'...  2.73 us
    pallas_call x1, Pallas kernels, packed(): pl.pallas_call(packing_kernel, out_shape=jax.ShapeDtypeStruct(chunks, que...  2.13 us
    pallas_call x1, Pallas kernels, piled(): pl.pallas_call(piling_kernel, out_shape=jax.ShapeDtypeStruct((groups, key...  1.55 us
  transfers between devices with their start and end apart: 9, of which 7 were waited for; matrix products, arithmetic and copies ran while one was open for 0% of the time, Pallas kernels for 3%

profile of v4, /device:TPU:6, one launch (start us, length us, event | category | flops | bytes accessed | tf_op | source)
XLA Modules:
  0.0 63.3 jit_solution(16592014594530178003)
XLA Ops:
  0.6 1.6 %shard_map.85 = bf16[8,32,256]{2,1,0:T(8,128)(2,1)} custom-call(bf16[32,1024]{1,0:T(8,128)(2,1)} %keys_ref.1, bf16[32,1024]{1,0:T(8,128)(2,1)} %values_ref.1), custom_call_target="tpu_custom_call" | custom-call | bytes 260000 | tf_op jit(solution)/shard_map/pallas_call | solution.py:260
  2.2 5.9 %all-to-all-start = ((bf16[8,32,256]{2,1,0:T(8,128)(2,1)}), bf16[8,32,256]{2,1,0:T(8,128)(2,1)S(1)}, u32[]{:S(2)}, u32[]{:S(2)}) async-start(bf16[8,32,256]{2,1,0:T(8,128)(2,1)} %shard_map.85), calls=%async_computation | async-start | bytes 262144 | tf_op jit(solution)/shard_map/all_to_all | solution.py:200
  8.1 2.1 %shard_map.84 = bf16[8,32,2048]{2,1,0:T(8,128)(2,1)} custom-call(bf16[32,8192]{1,0:T(8,128)(2,1)} %queries_ref.1, bf16[32,8192]{1,0:T(8,128)(2,1)} %grad_out_ref.1), custom_call_target="tpu_custom_call" | custom-call | bytes 2100000 | tf_op jit(solution)/shard_map/pallas_call | solution.py:235
  10.2 3.3 %all-to-all-done = bf16[8,32,256]{2,1,0:T(8,128)(2,1)S(1)} async-done(((bf16[8,32,256]{2,1,0:T(8,128)(2,1)}), bf16[8,32,256]{2,1,0:T(8,128)(2,1)S(1)}, u32[]{:S(2)}, u32[]{:S(2)}) %all-to-all-start) | async-done | bytes 131104 | tf_op jit(solution)/shard_map/all_to_all | solution.py:200
  13.5 4.7 %all-to-all-start.1 = ((bf16[8,32,2048]{2,1,0:T(8,128)(2,1)}), bf16[8,32,2048]{2,1,0:T(8,128)(2,1)S(1)}, u32[]{:S(2)}, u32[]{:S(2)}) async-start(bf16[8,32,2048]{2,1,0:T(8,128)(2,1)} %shard_map.84), calls=%async_computation.1 | async-start | bytes 2097152 | tf_op jit(solution)/shard_map/all_to_all | solution.py:200
  18.3 5.2 %collective-permute-start.1 = (bf16[256,256]{1,0:T(8,128)(2,1)S(1)}, bf16[256,256]{1,0:T(8,128)(2,1)S(1)}, u32[]{:S(2)}, u32[]{:S(2)}) collective-permute-start(bf16[256,256]{1,0:T(8,128)(2,1)S(1)} %bitcast.3), channel_id=1, source_target_pairs={{0,32},{8,40},{16,48},{24,56},{32,64},{40,72},{48,80},{56,88},{64,... | collective-permute-start | bytes 393224 | tf_op jit(solution)/shard_map/ppermute | solution.py:192
  23.5 3.8 %collective-permute-start = (bf16[256,256]{1,0:T(8,128)(2,1)S(1)}, bf16[256,256]{1,0:T(8,128)(2,1)S(1)}, u32[]{:S(2)}, u32[]{:S(2)}) collective-permute-start(bf16[256,256]{1,0:T(8,128)(2,1)S(1)} %bitcast.4), channel_id=1, source_target_pairs={{0,16},{8,24},{16,32},{24,40},{32,48},{40,56},{48,64},{56,72},{64,... | collective-permute-start | bytes 393224 | tf_op jit(solution)/shard_map/ppermute | solution.py:192
  27.3 5.9 %collective-permute-done.1.four_ref = bf16[256,256]{1,0:T(8,128)(2,1)S(1)} collective-permute-done((bf16[256,256]{1,0:T(8,128)(2,1)S(1)}, bf16[256,256]{1,0:T(8,128)(2,1)S(1)}, u32[]{:S(2)}, u32[]{:S(2)}) %collective-permute-start.1) | collective-permute-done | bytes 131104 | tf_op jit(solution)/shard_map/ppermute | solution.py:192
  33.2 0.0 copy-start
  33.2 0.1 collective-permute-start.3
  33.3 1.0 %collective-permute-done.two_ref = bf16[256,256]{1,0:T(8,128)(2,1)S(1)} collective-permute-done((bf16[256,256]{1,0:T(8,128)(2,1)S(1)}, bf16[256,256]{1,0:T(8,128)(2,1)S(1)}, u32[]{:S(2)}, u32[]{:S(2)}) %collective-permute-start) | collective-permute-done | bytes 131104 | tf_op jit(solution)/shard_map/ppermute | solution.py:192
  34.3 0.0 collective-permute-start.2
  34.3 0.4 collective-permute-done.3.their_other_ref
  34.7 1.0 %collective-permute-done.2.their_two_ref = bf16[256,256]{1,0:T(8,128)(2,1)S(1)} collective-permute-done((bf16[256,256]{1,0:T(8,128)(2,1)S(1)}, bf16[256,256]{1,0:T(8,128)(2,1)S(1)}, u32[]{:S(2)}, u32[]{:S(2)}) %collective-permute-start.2) | collective-permute-done | bytes 131104 | tf_op jit(solution)/shard_map/ppermute | solution.py:196
  35.7 0.0 all-to-all-done.1
  35.7 0.0 copy-done
  35.7 10.6 %shard_map.86 = (bf16[256,1024]{1,0:T(8,128)(2,1)}, bf16[256,1024]{1,0:T(8,128)(2,1)}, f32[256,768]{1,0:T(8,128)S(1)}, bf16[256,512]{1,0:T(8,128)(2,1)S(1)}) custom-call(s32[16]{0:T(128)S(1)} %copy-done, bf16[256,2048]{1,0:T(8,128)(2,1)S(1)} %bitcast.2, bf16[256,256]{1,0:T(8,128)(2,1)S(1)} %bitcast.6, bf16[256,256]{1,0:T(8,128)(2,1)S(1)} %collective-permute-done.two_ref, ...), custom_call_target="tpu_custom_call" | custom-call | flops 3000000000 | bytes 4000000 | tf_op jit(solution)/shard_map/pallas_call | solution.py:159
  46.2 0.1 collective-permute-start.4
  46.4 1.4 %collective-permute-done.4 = bf16[256,512]{1,0:T(8,128)(2,1)S(1)} collective-permute-done((bf16[256,512]{1,0:T(8,128)(2,1)S(1)}, bf16[256,512]{1,0:T(8,128)(2,1)S(1)}, u32[]{:S(2)}, u32[]{:S(2)}) %collective-permute-start.4) | collective-permute-done | bytes 262176 | tf_op jit(solution)/shard_map/ppermute | solution.py:196
  47.7 0.1 convert_element_type.18
  47.8 0.1 add_convert_fusion.2
  47.9 4.7 %collective-permute-start.5 = (bf16[256,256]{1,0:T(8,128)(2,1)S(1)}, bf16[256,256]{1,0:T(8,128)(2,1)S(1)}, u32[]{:S(2)}, u32[]{:S(2)}) collective-permute-start(bf16[256,256]{1,0:T(8,128)(2,1)S(1)} %get-tuple-element.16), channel_id=1, source_target_pairs={{16,0},{24,8},{32,16},{40,24},{48,32},{56,40},{64,48},{72,56},{80,... | collective-permute-start | bytes 393224 | tf_op jit(solution)/shard_map/ppermute | solution.py:192
  52.6 3.5 %collective-permute-start.6 = (bf16[256,256]{1,0:T(8,128)(2,1)S(1)}, bf16[256,256]{1,0:T(8,128)(2,1)S(1)}, u32[]{:S(2)}, u32[]{:S(2)}) collective-permute-start(bf16[256,256]{1,0:T(8,128)(2,1)S(1)} %get-tuple-element.17), channel_id=1, source_target_pairs={{32,0},{40,8},{48,16},{56,24},{64,32},{72,40},{80,48},{88,56},{96,... | collective-permute-start | bytes 393224 | tf_op jit(solution)/shard_map/ppermute | solution.py:192
  56.1 0.0 collective-permute-done.5
  56.1 6.5 %collective-permute-done.6 = bf16[256,256]{1,0:T(8,128)(2,1)S(1)} collective-permute-done((bf16[256,256]{1,0:T(8,128)(2,1)S(1)}, bf16[256,256]{1,0:T(8,128)(2,1)S(1)}, u32[]{:S(2)}, u32[]{:S(2)}) %collective-permute-start.6) | collective-permute-done | bytes 131104 | tf_op jit(solution)/shard_map/ppermute | solution.py:192
  62.6 0.1 add_convert_fusion
  62.7 0.7 %fusion = (bf16[256,128]{1,0:T(8,128)(2,1)}, bf16[256,128]{1,0:T(8,128)(2,1)}) fusion(bf16[256,256]{1,0:T(8,128)(2,1)S(1)} %add_convert_fusion), kind=kLoop, calls=%fused_computation.4 | loop fusion | bytes 262144 | tf_op jit(solution)/shard_map/slice | solution.py:291
  (1 shorter events, 0.0 us)
Async XLA Ops:
  2.2 11.3 %all-to-all-start = ((bf16[8,32,256]{2,1,0:T(8,128)(2,1)}), bf16[8,32,256]{2,1,0:T(8,128)(2,1)S(1)}, u32[]{:S(2)}, u32[]{:S(2)}) async-start(bf16[8,32,256]{2,1,0:T(8,128)(2,1)} %shard_map.85), calls=%async_computation | async-start | bytes 262144 | tf_op jit(solution)/shard_map/all_to_all | solution.py:200
  13.5 22.1 %all-to-all-start.1 = ((bf16[8,32,2048]{2,1,0:T(8,128)(2,1)}), bf16[8,32,2048]{2,1,0:T(8,128)(2,1)S(1)}, u32[]{:S(2)}, u32[]{:S(2)}) async-start(bf16[8,32,2048]{2,1,0:T(8,128)(2,1)} %shard_map.84), calls=%async_computation.1 | async-start | bytes 2097152 | tf_op jit(solution)/shard_map/all_to_all | solution.py:200
  18.3 14.9 %collective-permute-start.1 = (bf16[256,256]{1,0:T(8,128)(2,1)S(1)}, bf16[256,256]{1,0:T(8,128)(2,1)S(1)}, u32[]{:S(2)}, u32[]{:S(2)}) collective-permute-start(bf16[256,256]{1,0:T(8,128)(2,1)S(1)} %bitcast.3), channel_id=1, source_target_pairs={{0,32},{8,40},{16,48},{24,56},{32,64},{40,72},{48,80},{56,88},{64,... | collective-permute-start | bytes 393224 | tf_op jit(solution)/shard_map/ppermute | solution.py:192
  23.5 10.9 %collective-permute-start = (bf16[256,256]{1,0:T(8,128)(2,1)S(1)}, bf16[256,256]{1,0:T(8,128)(2,1)S(1)}, u32[]{:S(2)}, u32[]{:S(2)}) collective-permute-start(bf16[256,256]{1,0:T(8,128)(2,1)S(1)} %bitcast.4), channel_id=1, source_target_pairs={{0,16},{8,24},{16,32},{24,40},{32,48},{40,56},{48,64},{56,72},{64,... | collective-permute-start | bytes 393224 | tf_op jit(solution)/shard_map/ppermute | solution.py:192
  33.2 2.4 %copy-start = (s32[16]{0:T(128)S(1)}, s32[16]{0:T(128)}, u32[]{:S(2)}) copy-start(s32[16]{0:T(128)} %doc_ref.1) | copy-start | bytes 196
  33.2 1.4 %collective-permute-start.3 = (bf16[256,256]{1,0:T(8,128)(2,1)S(1)}, bf16[256,256]{1,0:T(8,128)(2,1)S(1)}, u32[]{:S(2)}, u32[]{:S(2)}) collective-permute-start(bf16[256,256]{1,0:T(8,128)(2,1)S(1)} %broadcast_select_fusion), channel_id=1, source_target_pairs={{0,8},{8,0},{16,24},{24,16},{32,40},{40,32},{48,56},{56,48},{64,72... | collective-permute-start | bytes 393224 | tf_op jit(solution)/shard_map/ppermute | solution.py:196
  34.3 1.3 %collective-permute-start.2 = (bf16[256,256]{1,0:T(8,128)(2,1)S(1)}, bf16[256,256]{1,0:T(8,128)(2,1)S(1)}, u32[]{:S(2)}, u32[]{:S(2)}) collective-permute-start(bf16[256,256]{1,0:T(8,128)(2,1)S(1)} %collective-permute-done.two_ref), channel_id=1, source_target_pairs={{0,8},{8,0},{16,24},{24,16},{32,40},{40,32},{48,56},{56,48},{64,72... | collective-permute-start | bytes 393224 | tf_op jit(solution)/shard_map/ppermute | solution.py:196
  46.2 1.5 %collective-permute-start.4 = (bf16[256,512]{1,0:T(8,128)(2,1)S(1)}, bf16[256,512]{1,0:T(8,128)(2,1)S(1)}, u32[]{:S(2)}, u32[]{:S(2)}) collective-permute-start(bf16[256,512]{1,0:T(8,128)(2,1)S(1)} %get-tuple-element.15), channel_id=1, source_target_pairs={{0,8},{8,0},{16,24},{24,16},{32,40},{40,32},{48,56},{56,48},{64,72... | collective-permute-start | bytes 786440 | tf_op jit(solution)/shard_map/ppermute | solution.py:196
  47.9 8.2 %collective-permute-start.5 = (bf16[256,256]{1,0:T(8,128)(2,1)S(1)}, bf16[256,256]{1,0:T(8,128)(2,1)S(1)}, u32[]{:S(2)}, u32[]{:S(2)}) collective-permute-start(bf16[256,256]{1,0:T(8,128)(2,1)S(1)} %get-tuple-element.16), channel_id=1, source_target_pairs={{16,0},{24,8},{32,16},{40,24},{48,32},{56,40},{64,48},{72,56},{80,... | collective-permute-start | bytes 393224 | tf_op jit(solution)/shard_map/ppermute | solution.py:192
  52.6 10.0 %collective-permute-start.6 = (bf16[256,256]{1,0:T(8,128)(2,1)S(1)}, bf16[256,256]{1,0:T(8,128)(2,1)S(1)}, u32[]{:S(2)}, u32[]{:S(2)}) collective-permute-start(bf16[256,256]{1,0:T(8,128)(2,1)S(1)} %get-tuple-element.17), channel_id=1, source_target_pairs={{32,0},{40,8},{48,16},{56,24},{64,32},{72,40},{80,48},{88,56},{96,... | collective-permute-start | bytes 393224 | tf_op jit(solution)/shard_map/ppermute | solution.py:192

commit v5 on v4

--- a/solution.py
+++ b/solution.py
@@ -1,3 +1,5 @@
+import functools
+
 import jax
 import jax.numpy as jnp
 from jax import lax
@@ -13,6 +15,7 @@
 EXP2_SCALE = SCALE * 1.4426950408889634
 WINDOW = 9
 REACH = 8
+REACHES = (2, 4, 6, 8)
 
 
 def document_start(doc_ref, block):
@@ -66,81 +69,138 @@
         )
 
     def over_sublanes(op, array):
-        return op(array.reshape(BLOCK // 8, 8, 2 * BLOCK), axis=0)
-
-    def pair_of_heads(pair):
-        column = pair * (2 * HD)
-        for half in range(2):
-            low, high = half * BLOCK, (half + REACH) * BLOCK
-            valid = [2 * here - 7 + half + w >= starts[half] for w in range(REACH - 1)]
-            q2 = stacked(qg_ref, half, column)
-            g2 = stacked(qg_ref, half, HEADS * HD + column)
-            qt, gt = q2.T, g2.T
-            qs[half, pl.ds(column, 2 * BLOCK), :] = q2
-            columns = pl.ds(column, 2 * BLOCK)
-            highest = None
-            for w in range(REACH):
-                at = low + w * BLOCK
-                score = jnp.dot(kw[at : at + BLOCK, :], qt, preferred_element_type=jnp.float32)
-                if w == REACH - 1:
-                    score = jnp.where(causal, score, -1e30)
-                scores[half, w * BLOCK : (w + 1) * BLOCK, :] = score
-                top = over_sublanes(jnp.max, score)
-                if w < REACH - 1:
-                    top = jnp.where(valid[w], top, -1e30)
-                highest = top if highest is None else jnp.maximum(highest, top)
-            shift = jnp.max(highest, axis=0, keepdims=True) * EXP2_SCALE
-            total = None
-            for w in range(REACH):
-                rows = pl.ds(w * BLOCK, BLOCK)
-                down = shift if w == REACH - 1 else jnp.where(valid[w], shift, 1e30)
-                weight = jnp.exp2(scores[half, rows, :] * EXP2_SCALE - down)
-                part = over_sublanes(jnp.sum, weight)
-                total = part if total is None else total + part
-                weights[half, rows, columns] = weight.astype(jnp.bfloat16)
-            inverse = 1.0 / jnp.sum(total, axis=0, keepdims=True)
+        return op(array.reshape(-1, 8, 2 * BLOCK), axis=0)
+
+    class Unit:
+        def __init__(self, number, reach):
+            self.pair, self.half = divmod(number, 2)
+            self.slot = number % 2
+            self.column = self.pair * 2 * HD
+            self.columns = pl.ds(self.column, 2 * BLOCK)
+            self.low = (self.half + REACH - reach) * BLOCK
+            self.high = (self.half + REACH) * BLOCK
+            self.rows = pl.ds((REACH - reach) * BLOCK, reach * BLOCK)
+
+        def valid(self, w):
+            return 2 * here - 7 + self.half + w >= starts[self.half]
+
+        def load(self):
+            q2 = stacked(qg_ref, self.half, self.column)
+            self.qt = q2.T
+            self.gt = stacked(qg_ref, self.half, HEADS * HD + self.column).T
+            qs[self.half, self.columns, :] = q2
+            self.highest = None
+
+        def score(self, w):
+            at = (self.half + w) * BLOCK
+            score = jnp.dot(kw[at : at + BLOCK, :], self.qt, preferred_element_type=jnp.float32)
+            if w == REACH - 1:
+                score = jnp.where(causal, score, -1e30)
+            scores[self.slot, w * BLOCK : (w + 1) * BLOCK, :] = score
+            top = over_sublanes(jnp.max, score)
+            if w < REACH - 1:
+                top = jnp.where(self.valid(w), top, -1e30)
+            self.highest = top if self.highest is None else jnp.maximum(self.highest, top)
+
+        def level(self):
+            self.shift = jnp.max(self.highest, axis=0, keepdims=True) * EXP2_SCALE
+            self.total = None
+
+        def weigh(self, w):
+            rows = pl.ds(w * BLOCK, BLOCK)
+            down = self.shift if w == REACH - 1 else jnp.where(self.valid(w), self.shift, 1e30)
+            weight = jnp.exp2(scores[self.slot, rows, :] * EXP2_SCALE - down)
+            part = over_sublanes(jnp.sum, weight)
+            self.total = part if self.total is None else self.total + part
+            weights[self.half, rows, self.columns] = weight.astype(jnp.bfloat16)
+
+        def attend(self):
+            inverse = 1.0 / jnp.sum(self.total, axis=0, keepdims=True)
             att_t = (
                 jnp.dot(
-                    vt[:, low:high], weights[half, :, columns], preferred_element_type=jnp.float32
+                    vt[:, self.low : self.high],
+                    weights[self.half, self.rows, self.columns],
+                    preferred_element_type=jnp.float32,
                 )
                 * inverse
             ).astype(jnp.bfloat16)
-            scaled_t = (gt.astype(jnp.float32) * inverse).astype(jnp.bfloat16)
-            gs[half, pl.ds(column, 2 * BLOCK), :] = scaled_t.T
-            delta = jnp.sum(
-                scaled_t.astype(jnp.float32) * att_t.astype(jnp.float32), axis=0, keepdims=True
+            self.scaled_t = (self.gt.astype(jnp.float32) * inverse).astype(jnp.bfloat16)
+            gs[self.half, self.columns, :] = self.scaled_t.T
+            self.delta = jnp.sum(
+                self.scaled_t.astype(jnp.float32) * att_t.astype(jnp.float32),
+                axis=0,
+                keepdims=True,
             )
-            for w in range(REACH):
-                at = low + w * BLOCK
-                rows = pl.ds(w * BLOCK, BLOCK)
-                grad = jnp.dot(
-                    vw[at : at + BLOCK, :], scaled_t, preferred_element_type=jnp.float32
-                )
-                grads[half, rows, columns] = (
-                    weights[half, rows, columns].astype(jnp.float32) * (grad - delta)
-                ).astype(jnp.bfloat16)
+            self.store(att_ref, att_t)
+
+        def grade(self, w):
+            at = (self.half + w) * BLOCK
+            rows = pl.ds(w * BLOCK, BLOCK)
+            grad = jnp.dot(
+                vw[at : at + BLOCK, :], self.scaled_t, preferred_element_type=jnp.float32
+            )
+            grads[self.half, rows, self.columns] = (
+                weights[self.half, rows, self.columns].astype(jnp.float32) * (grad - self.delta)
+            ).astype(jnp.bfloat16)
+
+        def finish(self):
             gq_t = (
                 jnp.dot(
-                    kt[:, low:high], grads[half, :, columns], preferred_element_type=jnp.float32
+                    kt[:, self.low : self.high],
+                    grads[self.half, self.rows, self.columns],
+                    preferred_element_type=jnp.float32,
                 )
                 * SCALE
             ).astype(jnp.bfloat16)
-            rows = pl.ds(half * BLOCK, BLOCK)
+            self.store(gq_ref, gq_t)
+
+        def store(self, ref, turned):
             for i in range(2):
-                out = pl.ds(column + i * HD, HD)
-                att_ref[rows, out] = att_t[:, i * BLOCK : (i + 1) * BLOCK].T
-                gq_ref[rows, out] = gq_t[:, i * BLOCK : (i + 1) * BLOCK].T
-
-    for pair in range(HEADS // 2):
-        pair_of_heads(pair)
-    for out, left, right in ((dv, weights, gs), (dk, grads, qs)):
-        for half in range(2):
-            added = jnp.dot(left[half], right[half], preferred_element_type=jnp.float32)
-            if half == 0:
-                out[0:1024, :] = added
-                out[1024:1152, :] = jnp.zeros((BLOCK, HD), jnp.float32)
-            else:
-                out[128:1152, :] += added
+                ref[
+                    pl.ds(self.half * BLOCK, BLOCK), pl.ds(self.column + i * HD, HD)
+                ] = turned[:, i * BLOCK : (i + 1) * BLOCK].T
+
+    def work(reach):
+        units = [Unit(number, reach) for number in range(HEADS)]
+        for step in range(len(units) + 2):
+            first, second, third = (
+                units[step - lag] if 0 <= step - lag < len(units) else None for lag in range(3)
+            )
+            if first:
+                first.load()
+            if second:
+                second.level()
+            for w in range(REACH - reach, REACH):
+                if first:
+                    first.score(w)
+                if second:
+                    second.weigh(w)
+                if third:
+                    third.grade(w)
+            if second:
+                second.attend()
+            if third:
+                third.finish()
+        begin = (REACH - reach) * BLOCK
+        for out, left, right in ((dv, weights, gs), (dk, grads, qs)):
+            for half in range(2):
+                added = jnp.dot(
+                    left[half, begin : REACH * BLOCK, :],
+                    right[half],
+                    preferred_element_type=jnp.float32,
+                )
+                if half == 0:
+                    if begin:
+                        out[0:begin, :] = jnp.zeros((begin, HD), jnp.float32)
+                    out[begin : REACH * BLOCK, :] = added
+                    out[REACH * BLOCK :, :] = jnp.zeros((BLOCK, HD), jnp.float32)
+                else:
+                    out[begin + BLOCK :, :] += added
+
+    needed = jnp.maximum(2 * here - starts[0], 2 * here + 1 - starts[1]) + 1
+    for number, reach in enumerate(REACHES):
+        below = REACHES[number - 1] if number else 0
+        pl.when((needed > below) & (needed <= reach))(functools.partial(work, reach))
 
     for part, (total, factor) in enumerate(((dk, SCALE), (dv, None))):
         scaled = total[...] if factor is None else total[...] * factor

time: 64.2 us -> 61.6 us (0.960); the launches traced: 63.3 us -> 62.2 us
  Pallas kernels: 14.2 us -> 10.4 us
  starting transfers between devices: 28.1 us -> 29.5 us
  waiting for transfers between devices: 19.4 us -> 20.7 us
    pallas_call x1, Pallas kernels: 10.6 us -> 6.68 us  [attention(): pl.pallas_call(attention_kernel, out_shape=(jax.ShapeDtypeStruct((ROWS, H...]
    ppermute x4, starting transfers between devices: 17.1 us -> 18.7 us  [shifted(): return lax.ppermute(block, 'seq', route)]
    ppermute x4, waiting for transfers between devices: 13.4 us -> 14.6 us  [shifted(): return lax.ppermute(block, 'seq', route)]
  transfers between devices with their start and end apart: 9 -> 9, of which waited for: 7 -> 8; matrix products, arithmetic and copies ran while one was open for 0% -> 0% of each run, Pallas kernels for 3% -> 3%
where the time goes in v5:
time: 61.6 us; the launch traced here: 62.2 us
  starting transfers between devices  29.5 us (48%)
  waiting for transfers between devices  20.7 us (34%)
  Pallas kernels  10.4 us (17%)
  between operations  0.72 us (1%)
  local copies, waits for them, and re-layouts  0.67 us (1%)
    ppermute x4, starting transfers between devices, shifted(): return lax.ppermute(block, 'seq', route)  18.7 us
    ppermute x4, waiting for transfers between devices, shifted(): return lax.ppermute(block, 'seq', route)  14.6 us
    all_to_all x2, starting transfers between devices, exchanged(): lax.all_to_all(chunks, 'head', split_axis=0, concat_axis=0, tiled=True)  10.7 us
    pallas_call x1, Pallas kernels, attention(): pl.pallas_call(attention_kernel, out_shape=(jax.ShapeDtypeStruct((ROWS, H...  6.68 us
    all_to_all x2, waiting for transfers between devices, exchanged(): lax.all_to_all(chunks, 'head', split_axis=0, concat_axis=0, tiled=True)  3.28 us
    ppermute x3, waiting for transfers between devices, partners(): lax.ppermute(block, 'seq', [(i, i ^ 1) for i in range(lax.axis_size('seq'...  2.88 us
    pallas_call x1, Pallas kernels, packed(): pl.pallas_call(packing_kernel, out_shape=jax.ShapeDtypeStruct(chunks, que...  2.13 us
    pallas_call x1, Pallas kernels, piled(): pl.pallas_call(piling_kernel, out_shape=jax.ShapeDtypeStruct((groups, key...  1.55 us
  transfers between devices with their start and end apart: 9, of which 8 were waited for; matrix products, arithmetic and copies ran while one was open for 0% of the time, Pallas kernels for 3%

profile of v5, /device:TPU:6, one launch (start us, length us, event | category | flops | bytes accessed | tf_op | source)
XLA Modules:
  0.0 62.2 jit_solution(304428251833148849)
XLA Ops:
  0.6 1.6 %shard_map.85 = bf16[8,32,256]{2,1,0:T(8,128)(2,1)} custom-call(bf16[32,1024]{1,0:T(8,128)(2,1)} %keys_ref.1, bf16[32,1024]{1,0:T(8,128)(2,1)} %values_ref.1), custom_call_target="tpu_custom_call" | custom-call | bytes 260000 | tf_op jit(solution)/shard_map/pallas_call | solution.py:320
  2.2 5.9 %all-to-all-start = ((bf16[8,32,256]{2,1,0:T(8,128)(2,1)}), bf16[8,32,256]{2,1,0:T(8,128)(2,1)S(1)}, u32[]{:S(2)}, u32[]{:S(2)}) async-start(bf16[8,32,256]{2,1,0:T(8,128)(2,1)} %shard_map.85), calls=%async_computation | async-start | bytes 262144 | tf_op jit(solution)/shard_map/all_to_all | solution.py:260
  8.1 2.1 %shard_map.84 = bf16[8,32,2048]{2,1,0:T(8,128)(2,1)} custom-call(bf16[32,8192]{1,0:T(8,128)(2,1)} %queries_ref.1, bf16[32,8192]{1,0:T(8,128)(2,1)} %grad_out_ref.1), custom_call_target="tpu_custom_call" | custom-call | bytes 2100000 | tf_op jit(solution)/shard_map/pallas_call | solution.py:295
  10.2 3.3 %all-to-all-done = bf16[8,32,256]{2,1,0:T(8,128)(2,1)S(1)} async-done(((bf16[8,32,256]{2,1,0:T(8,128)(2,1)}), bf16[8,32,256]{2,1,0:T(8,128)(2,1)S(1)}, u32[]{:S(2)}, u32[]{:S(2)}) %all-to-all-start) | async-done | bytes 131104 | tf_op jit(solution)/shard_map/all_to_all | solution.py:260
  13.5 4.7 %all-to-all-start.1 = ((bf16[8,32,2048]{2,1,0:T(8,128)(2,1)}), bf16[8,32,2048]{2,1,0:T(8,128)(2,1)S(1)}, u32[]{:S(2)}, u32[]{:S(2)}) async-start(bf16[8,32,2048]{2,1,0:T(8,128)(2,1)} %shard_map.84), calls=%async_computation.1 | async-start | bytes 2097152 | tf_op jit(solution)/shard_map/all_to_all | solution.py:260
  18.3 5.2 %collective-permute-start.1 = (bf16[256,256]{1,0:T(8,128)(2,1)S(1)}, bf16[256,256]{1,0:T(8,128)(2,1)S(1)}, u32[]{:S(2)}, u32[]{:S(2)}) collective-permute-start(bf16[256,256]{1,0:T(8,128)(2,1)S(1)} %bitcast.3), channel_id=1, source_target_pairs={{0,32},{8,40},{16,48},{24,56},{32,64},{40,72},{48,80},{56,88},{64,... | collective-permute-start | bytes 393224 | tf_op jit(solution)/shard_map/ppermute | solution.py:252
  23.5 3.8 %collective-permute-start = (bf16[256,256]{1,0:T(8,128)(2,1)S(1)}, bf16[256,256]{1,0:T(8,128)(2,1)S(1)}, u32[]{:S(2)}, u32[]{:S(2)}) collective-permute-start(bf16[256,256]{1,0:T(8,128)(2,1)S(1)} %bitcast.4), channel_id=1, source_target_pairs={{0,16},{8,24},{16,32},{24,40},{32,48},{40,56},{48,64},{56,72},{64,... | collective-permute-start | bytes 393224 | tf_op jit(solution)/shard_map/ppermute | solution.py:252
  27.3 5.9 %collective-permute-done.1.four_ref = bf16[256,256]{1,0:T(8,128)(2,1)S(1)} collective-permute-done((bf16[256,256]{1,0:T(8,128)(2,1)S(1)}, bf16[256,256]{1,0:T(8,128)(2,1)S(1)}, u32[]{:S(2)}, u32[]{:S(2)}) %collective-permute-start.1) | collective-permute-done | bytes 131104 | tf_op jit(solution)/shard_map/ppermute | solution.py:252
  33.2 0.0 copy-start
  33.2 0.1 collective-permute-start.3
  33.3 1.0 %collective-permute-done.two_ref = bf16[256,256]{1,0:T(8,128)(2,1)S(1)} collective-permute-done((bf16[256,256]{1,0:T(8,128)(2,1)S(1)}, bf16[256,256]{1,0:T(8,128)(2,1)S(1)}, u32[]{:S(2)}, u32[]{:S(2)}) %collective-permute-start) | collective-permute-done | bytes 131104 | tf_op jit(solution)/shard_map/ppermute | solution.py:252
  34.3 0.0 collective-permute-start.2
  34.3 0.4 collective-permute-done.3.their_other_ref
  34.7 1.0 %collective-permute-done.2.their_two_ref = bf16[256,256]{1,0:T(8,128)(2,1)S(1)} collective-permute-done((bf16[256,256]{1,0:T(8,128)(2,1)S(1)}, bf16[256,256]{1,0:T(8,128)(2,1)S(1)}, u32[]{:S(2)}, u32[]{:S(2)}) %collective-permute-start.2) | collective-permute-done | bytes 131104 | tf_op jit(solution)/shard_map/ppermute | solution.py:256
  35.7 0.0 all-to-all-done.1
  35.7 0.0 copy-done
  35.7 6.7 %shard_map.86 = (bf16[256,1024]{1,0:T(8,128)(2,1)}, bf16[256,1024]{1,0:T(8,128)(2,1)}, f32[256,768]{1,0:T(8,128)S(1)}, bf16[256,512]{1,0:T(8,128)(2,1)S(1)}) custom-call(s32[16]{0:T(128)S(1)} %copy-done, bf16[256,2048]{1,0:T(8,128)(2,1)S(1)} %bitcast.2, bf16[256,256]{1,0:T(8,128)(2,1)S(1)} %bitcast.6, bf16[256,256]{1,0:T(8,128)(2,1)S(1)} %collective-permute-done.two_ref, ...), custom_call_target="tpu_custom_call" | custom-call | flops 3000000000 | bytes 4000000 | tf_op jit(solution)/shard_map/pallas_call | solution.py:219
  42.3 0.0 collective-permute-start.4
  42.3 1.5 %collective-permute-done.4 = bf16[256,512]{1,0:T(8,128)(2,1)S(1)} collective-permute-done((bf16[256,512]{1,0:T(8,128)(2,1)S(1)}, bf16[256,512]{1,0:T(8,128)(2,1)S(1)}, u32[]{:S(2)}, u32[]{:S(2)}) %collective-permute-start.4) | collective-permute-done | bytes 262176 | tf_op jit(solution)/shard_map/ppermute | solution.py:256
  43.9 0.1 convert_element_type.18
  43.9 0.1 add_convert_fusion.2
  44.0 7.8 %collective-permute-start.5 = (bf16[256,256]{1,0:T(8,128)(2,1)S(1)}, bf16[256,256]{1,0:T(8,128)(2,1)S(1)}, u32[]{:S(2)}, u32[]{:S(2)}) collective-permute-start(bf16[256,256]{1,0:T(8,128)(2,1)S(1)} %get-tuple-element.16), channel_id=1, source_target_pairs={{16,0},{24,8},{32,16},{40,24},{48,32},{56,40},{64,48},{72,56},{80,... | collective-permute-start | bytes 393224 | tf_op jit(solution)/shard_map/ppermute | solution.py:252
  51.8 1.9 %collective-permute-start.6 = (bf16[256,256]{1,0:T(8,128)(2,1)S(1)}, bf16[256,256]{1,0:T(8,128)(2,1)S(1)}, u32[]{:S(2)}, u32[]{:S(2)}) collective-permute-start(bf16[256,256]{1,0:T(8,128)(2,1)S(1)} %get-tuple-element.17), channel_id=1, source_target_pairs={{32,0},{40,8},{48,16},{56,24},{64,32},{72,40},{80,48},{88,56},{96,... | collective-permute-start | bytes 393224 | tf_op jit(solution)/shard_map/ppermute | solution.py:252
  53.8 3.5 %collective-permute-done.5 = bf16[256,256]{1,0:T(8,128)(2,1)S(1)} collective-permute-done((bf16[256,256]{1,0:T(8,128)(2,1)S(1)}, bf16[256,256]{1,0:T(8,128)(2,1)S(1)}, u32[]{:S(2)}, u32[]{:S(2)}) %collective-permute-start.5) | collective-permute-done | bytes 131104 | tf_op jit(solution)/shard_map/ppermute | solution.py:252
  57.2 4.2 %collective-permute-done.6 = bf16[256,256]{1,0:T(8,128)(2,1)S(1)} collective-permute-done((bf16[256,256]{1,0:T(8,128)(2,1)S(1)}, bf16[256,256]{1,0:T(8,128)(2,1)S(1)}, u32[]{:S(2)}, u32[]{:S(2)}) %collective-permute-start.6) | collective-permute-done | bytes 131104 | tf_op jit(solution)/shard_map/ppermute | solution.py:252
  61.5 0.1 add_convert_fusion
  61.5 0.7 %fusion = (bf16[256,128]{1,0:T(8,128)(2,1)}, bf16[256,128]{1,0:T(8,128)(2,1)}) fusion(bf16[256,256]{1,0:T(8,128)(2,1)S(1)} %add_convert_fusion), kind=kLoop, calls=%fused_computation.4 | loop fusion | bytes 262144 | tf_op jit(solution)/shard_map/slice | solution.py:351
  (1 shorter events, 0.0 us)
Async XLA Ops:
  2.2 11.3 %all-to-all-start = ((bf16[8,32,256]{2,1,0:T(8,128)(2,1)}), bf16[8,32,256]{2,1,0:T(8,128)(2,1)S(1)}, u32[]{:S(2)}, u32[]{:S(2)}) async-start(bf16[8,32,256]{2,1,0:T(8,128)(2,1)} %shard_map.85), calls=%async_computation | async-start | bytes 262144 | tf_op jit(solution)/shard_map/all_to_all | solution.py:260
  13.5 22.1 %all-to-all-start.1 = ((bf16[8,32,2048]{2,1,0:T(8,128)(2,1)}), bf16[8,32,2048]{2,1,0:T(8,128)(2,1)S(1)}, u32[]{:S(2)}, u32[]{:S(2)}) async-start(bf16[8,32,2048]{2,1,0:T(8,128)(2,1)} %shard_map.84), calls=%async_computation.1 | async-start | bytes 2097152 | tf_op jit(solution)/shard_map/all_to_all | solution.py:260
  18.3 14.9 %collective-permute-start.1 = (bf16[256,256]{1,0:T(8,128)(2,1)S(1)}, bf16[256,256]{1,0:T(8,128)(2,1)S(1)}, u32[]{:S(2)}, u32[]{:S(2)}) collective-permute-start(bf16[256,256]{1,0:T(8,128)(2,1)S(1)} %bitcast.3), channel_id=1, source_target_pairs={{0,32},{8,40},{16,48},{24,56},{32,64},{40,72},{48,80},{56,88},{64,... | collective-permute-start | bytes 393224 | tf_op jit(solution)/shard_map/ppermute | solution.py:252
  23.5 10.9 %collective-permute-start = (bf16[256,256]{1,0:T(8,128)(2,1)S(1)}, bf16[256,256]{1,0:T(8,128)(2,1)S(1)}, u32[]{:S(2)}, u32[]{:S(2)}) collective-permute-start(bf16[256,256]{1,0:T(8,128)(2,1)S(1)} %bitcast.4), channel_id=1, source_target_pairs={{0,16},{8,24},{16,32},{24,40},{32,48},{40,56},{48,64},{56,72},{64,... | collective-permute-start | bytes 393224 | tf_op jit(solution)/shard_map/ppermute | solution.py:252
  33.2 2.4 %copy-start = (s32[16]{0:T(128)S(1)}, s32[16]{0:T(128)}, u32[]{:S(2)}) copy-start(s32[16]{0:T(128)} %doc_ref.1) | copy-start | bytes 196
  33.2 1.4 %collective-permute-start.3 = (bf16[256,256]{1,0:T(8,128)(2,1)S(1)}, bf16[256,256]{1,0:T(8,128)(2,1)S(1)}, u32[]{:S(2)}, u32[]{:S(2)}) collective-permute-start(bf16[256,256]{1,0:T(8,128)(2,1)S(1)} %broadcast_select_fusion), channel_id=1, source_target_pairs={{0,8},{8,0},{16,24},{24,16},{32,40},{40,32},{48,56},{56,48},{64,72... | collective-permute-start | bytes 393224 | tf_op jit(solution)/shard_map/ppermute | solution.py:256
  34.3 1.3 %collective-permute-start.2 = (bf16[256,256]{1,0:T(8,128)(2,1)S(1)}, bf16[256,256]{1,0:T(8,128)(2,1)S(1)}, u32[]{:S(2)}, u32[]{:S(2)}) collective-permute-start(bf16[256,256]{1,0:T(8,128)(2,1)S(1)} %collective-permute-done.two_ref), channel_id=1, source_target_pairs={{0,8},{8,0},{16,24},{24,16},{32,40},{40,32},{48,56},{56,48},{64,72... | collective-permute-start | bytes 393224 | tf_op jit(solution)/shard_map/ppermute | solution.py:256
  42.3 1.5 %collective-permute-start.4 = (bf16[256,512]{1,0:T(8,128)(2,1)S(1)}, bf16[256,512]{1,0:T(8,128)(2,1)S(1)}, u32[]{:S(2)}, u32[]{:S(2)}) collective-permute-start(bf16[256,512]{1,0:T(8,128)(2,1)S(1)} %get-tuple-element.15), channel_id=1, source_target_pairs={{0,8},{8,0},{16,24},{24,16},{32,40},{40,32},{48,56},{56,48},{64,72... | collective-permute-start | bytes 786440 | tf_op jit(solution)/shard_map/ppermute | solution.py:256
  44.0 13.2 %collective-permute-start.5 = (bf16[256,256]{1,0:T(8,128)(2,1)S(1)}, bf16[256,256]{1,0:T(8,128)(2,1)S(1)}, u32[]{:S(2)}, u32[]{:S(2)}) collective-permute-start(bf16[256,256]{1,0:T(8,128)(2,1)S(1)} %get-tuple-element.16), channel_id=1, source_target_pairs={{16,0},{24,8},{32,16},{40,24},{48,32},{56,40},{64,48},{72,56},{80,... | collective-permute-start | bytes 393224 | tf_op jit(solution)/shard_map/ppermute | solution.py:252
  51.8 9.6 %collective-permute-start.6 = (bf16[256,256]{1,0:T(8,128)(2,1)S(1)}, bf16[256,256]{1,0:T(8,128)(2,1)S(1)}, u32[]{:S(2)}, u32[]{:S(2)}) collective-permute-start(bf16[256,256]{1,0:T(8,128)(2,1)S(1)} %get-tuple-element.17), channel_id=1, source_target_pairs={{32,0},{40,8},{48,16},{56,24},{64,32},{72,40},{80,48},{88,56},{96,... | collective-permute-start | bytes 393224 | tf_op jit(solution)/shard_map/ppermute | solution.py:252

commit v6 on v5

--- a/solution.py
+++ b/solution.py
@@ -343,11 +343,8 @@
     for_here = kept[:, 0:256] + jnp.where(odd, 0.0, one)
     for_two = (kept[:, 256:512] + jnp.where(odd, one, three)).astype(jnp.bfloat16)
     for_four = (kept[:, 512:768] + jnp.where(odd, three, 0.0)).astype(jnp.bfloat16)
-    total = (
-        for_here
-        + shifted(for_two, -2).astype(jnp.float32)
-        + shifted(for_four, -4).astype(jnp.float32)
-    ).astype(jnp.bfloat16)
+    with_four = lax.optimization_barrier(for_here + shifted(for_four, -4).astype(jnp.float32))
+    total = (with_four + shifted(for_two, -2).astype(jnp.float32)).astype(jnp.bfloat16)
     return attended, grad_queries, total[:, 0:128], total[:, 128:256]
 
 

time: 61.6 us -> 59.9 us (0.972)
  waiting for transfers between devices: 20.7 us -> 18.2 us
  Pallas kernels: 10.4 us -> 11.9 us
  starting transfers between devices: 29.5 us -> 28.4 us
    ppermute x4, waiting for transfers between devices: 14.6 us -> 12 us  [shifted(): return lax.ppermute(block, 'seq', route)]
    pallas_call x1, Pallas kernels: 6.68 us -> 8.23 us  [attention(): pl.pallas_call(attention_kernel, out_shape=(jax.ShapeDtypeStruct((ROWS, H...]
    ppermute x4, starting transfers between devices: 18.7 us -> 17.6 us  [shifted(): return lax.ppermute(block, 'seq', route)]
  transfers between devices with their start and end apart: 9 -> 9, of which waited for: 8 -> 8; matrix products, arithmetic and copies ran while one was open for 0% -> 0% of each run, Pallas kernels for 3% -> 4%
where the time goes in v6:
time: 59.9 us; the launch traced here: 60.1 us
  starting transfers between devices  28.4 us (47%)
  waiting for transfers between devices  18.2 us (30%)
  Pallas kernels  11.9 us (20%)
  between operations  0.72 us (1%)
  local copies, waits for them, and re-layouts  0.67 us (1%)
    ppermute x4, starting transfers between devices, shifted(): return lax.ppermute(block, 'seq', route)  17.6 us
    ppermute x4, waiting for transfers between devices, shifted(): return lax.ppermute(block, 'seq', route)  12 us
    all_to_all x2, starting transfers between devices, exchanged(): lax.all_to_all(chunks, 'head', split_axis=0, concat_axis=0, tiled=True)  10.7 us
    pallas_call x1, Pallas kernels, attention(): pl.pallas_call(attention_kernel, out_shape=(jax.ShapeDtypeStruct((ROWS, H...  8.23 us
    all_to_all x2, waiting for transfers between devices, exchanged(): lax.all_to_all(chunks, 'head', split_axis=0, concat_axis=0, tiled=True)  3.28 us
    ppermute x3, waiting for transfers between devices, partners(): lax.ppermute(block, 'seq', [(i, i ^ 1) for i in range(lax.axis_size('seq'...  2.88 us
    pallas_call x1, Pallas kernels, packed(): pl.pallas_call(packing_kernel, out_shape=jax.ShapeDtypeStruct(chunks, que...  2.13 us
    pallas_call x1, Pallas kernels, piled(): pl.pallas_call(piling_kernel, out_shape=jax.ShapeDtypeStruct((groups, key...  1.55 us
  transfers between devices with their start and end apart: 9, of which 8 were waited for; matrix products, arithmetic and copies ran while one was open for 0% of the time, Pallas kernels for 4%

profile of v6, /device:TPU:6, one launch (start us, length us, event | category | flops | bytes accessed | tf_op | source)
XLA Modules:
  0.0 60.1 jit_solution(12028667967041890896)
XLA Ops:
  0.6 1.6 %shard_map.85 = bf16[8,32,256]{2,1,0:T(8,128)(2,1)} custom-call(bf16[32,1024]{1,0:T(8,128)(2,1)} %keys_ref.1, bf16[32,1024]{1,0:T(8,128)(2,1)} %values_ref.1), custom_call_target="tpu_custom_call" | custom-call | bytes 260000 | tf_op jit(solution)/shard_map/pallas_call | solution.py:320
  2.2 5.9 %all-to-all-start = ((bf16[8,32,256]{2,1,0:T(8,128)(2,1)}), bf16[8,32,256]{2,1,0:T(8,128)(2,1)S(1)}, u32[]{:S(2)}, u32[]{:S(2)}) async-start(bf16[8,32,256]{2,1,0:T(8,128)(2,1)} %shard_map.85), calls=%async_computation | async-start | bytes 262144 | tf_op jit(solution)/shard_map/all_to_all | solution.py:260
  8.1 2.1 %shard_map.84 = bf16[8,32,2048]{2,1,0:T(8,128)(2,1)} custom-call(bf16[32,8192]{1,0:T(8,128)(2,1)} %queries_ref.1, bf16[32,8192]{1,0:T(8,128)(2,1)} %grad_out_ref.1), custom_call_target="tpu_custom_call" | custom-call | bytes 2100000 | tf_op jit(solution)/shard_map/pallas_call | solution.py:295
  10.2 3.3 %all-to-all-done = bf16[8,32,256]{2,1,0:T(8,128)(2,1)S(1)} async-done(((bf16[8,32,256]{2,1,0:T(8,128)(2,1)}), bf16[8,32,256]{2,1,0:T(8,128)(2,1)S(1)}, u32[]{:S(2)}, u32[]{:S(2)}) %all-to-all-start) | async-done | bytes 131104 | tf_op jit(solution)/shard_map/all_to_all | solution.py:260
  13.5 4.7 %all-to-all-start.1 = ((bf16[8,32,2048]{2,1,0:T(8,128)(2,1)}), bf16[8,32,2048]{2,1,0:T(8,128)(2,1)S(1)}, u32[]{:S(2)}, u32[]{:S(2)}) async-start(bf16[8,32,2048]{2,1,0:T(8,128)(2,1)} %shard_map.84), calls=%async_computation.1 | async-start | bytes 2097152 | tf_op jit(solution)/shard_map/all_to_all | solution.py:260
  18.3 5.2 %collective-permute-start.1 = (bf16[256,256]{1,0:T(8,128)(2,1)S(1)}, bf16[256,256]{1,0:T(8,128)(2,1)S(1)}, u32[]{:S(2)}, u32[]{:S(2)}) collective-permute-start(bf16[256,256]{1,0:T(8,128)(2,1)S(1)} %bitcast.3), channel_id=1, source_target_pairs={{0,32},{8,40},{16,48},{24,56},{32,64},{40,72},{48,80},{56,88},{64,... | collective-permute-start | bytes 393224 | tf_op jit(solution)/shard_map/ppermute | solution.py:252
  23.5 3.8 %collective-permute-start = (bf16[256,256]{1,0:T(8,128)(2,1)S(1)}, bf16[256,256]{1,0:T(8,128)(2,1)S(1)}, u32[]{:S(2)}, u32[]{:S(2)}) collective-permute-start(bf16[256,256]{1,0:T(8,128)(2,1)S(1)} %bitcast.4), channel_id=1, source_target_pairs={{0,16},{8,24},{16,32},{24,40},{32,48},{40,56},{48,64},{56,72},{64,... | collective-permute-start | bytes 393224 | tf_op jit(solution)/shard_map/ppermute | solution.py:252
  27.3 5.9 %collective-permute-done.1.four_ref = bf16[256,256]{1,0:T(8,128)(2,1)S(1)} collective-permute-done((bf16[256,256]{1,0:T(8,128)(2,1)S(1)}, bf16[256,256]{1,0:T(8,128)(2,1)S(1)}, u32[]{:S(2)}, u32[]{:S(2)}) %collective-permute-start.1) | collective-permute-done | bytes 131104 | tf_op jit(solution)/shard_map/ppermute | solution.py:252
  33.2 0.0 copy-start
  33.2 0.1 collective-permute-start.3
  33.3 1.0 %collective-permute-done.two_ref = bf16[256,256]{1,0:T(8,128)(2,1)S(1)} collective-permute-done((bf16[256,256]{1,0:T(8,128)(2,1)S(1)}, bf16[256,256]{1,0:T(8,128)(2,1)S(1)}, u32[]{:S(2)}, u32[]{:S(2)}) %collective-permute-start) | collective-permute-done | bytes 131104 | tf_op jit(solution)/shard_map/ppermute | solution.py:252
  34.3 0.0 collective-permute-start.2
  34.3 0.4 collective-permute-done.3.their_other_ref
  34.7 1.0 %collective-permute-done.2.their_two_ref = bf16[256,256]{1,0:T(8,128)(2,1)S(1)} collective-permute-done((bf16[256,256]{1,0:T(8,128)(2,1)S(1)}, bf16[256,256]{1,0:T(8,128)(2,1)S(1)}, u32[]{:S(2)}, u32[]{:S(2)}) %collective-permute-start.2) | collective-permute-done | bytes 131104 | tf_op jit(solution)/shard_map/ppermute | solution.py:256
  35.7 0.0 all-to-all-done.1
  35.7 0.0 copy-done
  35.7 8.2 %shard_map.86 = (bf16[256,1024]{1,0:T(8,128)(2,1)}, bf16[256,1024]{1,0:T(8,128)(2,1)}, f32[256,768]{1,0:T(8,128)S(1)}, bf16[256,512]{1,0:T(8,128)(2,1)S(1)}) custom-call(s32[16]{0:T(128)S(1)} %copy-done, bf16[256,2048]{1,0:T(8,128)(2,1)S(1)} %bitcast.2, bf16[256,256]{1,0:T(8,128)(2,1)S(1)} %bitcast.6, bf16[256,256]{1,0:T(8,128)(2,1)S(1)} %collective-permute-done.two_ref, ...), custom_call_target="tpu_custom_call" | custom-call | flops 3000000000 | bytes 4000000 | tf_op jit(solution)/shard_map/pallas_call | solution.py:219
  43.9 0.0 collective-permute-start.4
  43.9 1.5 %collective-permute-done.4 = bf16[256,512]{1,0:T(8,128)(2,1)S(1)} collective-permute-done((bf16[256,512]{1,0:T(8,128)(2,1)S(1)}, bf16[256,512]{1,0:T(8,128)(2,1)S(1)}, u32[]{:S(2)}, u32[]{:S(2)}) %collective-permute-start.4) | collective-permute-done | bytes 262176 | tf_op jit(solution)/shard_map/ppermute | solution.py:256
  45.4 0.1 convert_element_type.18
  45.5 0.1 add_convert_fusion.1
  45.6 6.7 %collective-permute-start.5 = (bf16[256,256]{1,0:T(8,128)(2,1)S(1)}, bf16[256,256]{1,0:T(8,128)(2,1)S(1)}, u32[]{:S(2)}, u32[]{:S(2)}) collective-permute-start(bf16[256,256]{1,0:T(8,128)(2,1)S(1)} %get-tuple-element.17), channel_id=1, source_target_pairs={{32,0},{40,8},{48,16},{56,24},{64,32},{72,40},{80,48},{88,56},{96,... | collective-permute-start | bytes 393224 | tf_op jit(solution)/shard_map/ppermute | solution.py:252
  52.3 1.9 %collective-permute-start.6 = (bf16[256,256]{1,0:T(8,128)(2,1)S(1)}, bf16[256,256]{1,0:T(8,128)(2,1)S(1)}, u32[]{:S(2)}, u32[]{:S(2)}) collective-permute-start(bf16[256,256]{1,0:T(8,128)(2,1)S(1)} %get-tuple-element.16), channel_id=1, source_target_pairs={{16,0},{24,8},{32,16},{40,24},{48,32},{56,40},{64,48},{72,56},{80,... | collective-permute-start | bytes 393224 | tf_op jit(solution)/shard_map/ppermute | solution.py:252
  54.2 1.9 %collective-permute-done.5 = bf16[256,256]{1,0:T(8,128)(2,1)S(1)} collective-permute-done((bf16[256,256]{1,0:T(8,128)(2,1)S(1)}, bf16[256,256]{1,0:T(8,128)(2,1)S(1)}, u32[]{:S(2)}, u32[]{:S(2)}) %collective-permute-start.5) | collective-permute-done | bytes 131104 | tf_op jit(solution)/shard_map/ppermute | solution.py:252
  56.1 0.1 convert_add_fusion
  56.2 3.3 %collective-permute-done.6 = bf16[256,256]{1,0:T(8,128)(2,1)S(1)} collective-permute-done((bf16[256,256]{1,0:T(8,128)(2,1)S(1)}, bf16[256,256]{1,0:T(8,128)(2,1)S(1)}, u32[]{:S(2)}, u32[]{:S(2)}) %collective-permute-start.6) | collective-permute-done | bytes 131104 | tf_op jit(solution)/shard_map/ppermute | solution.py:252
  59.5 0.7 %fusion = (bf16[256,128]{1,0:T(8,128)(2,1)}, bf16[256,128]{1,0:T(8,128)(2,1)}) fusion(bf16[256,256]{1,0:T(8,128)(2,1)S(1)} %add_convert_fusion), kind=kLoop, calls=%fused_computation.5 | loop fusion | bytes 262144 | tf_op jit(solution)/shard_map/slice | solution.py:348
  (2 shorter events, 0.0 us)
Async XLA Ops:
  2.2 11.3 %all-to-all-start = ((bf16[8,32,256]{2,1,0:T(8,128)(2,1)}), bf16[8,32,256]{2,1,0:T(8,128)(2,1)S(1)}, u32[]{:S(2)}, u32[]{:S(2)}) async-start(bf16[8,32,256]{2,1,0:T(8,128)(2,1)} %shard_map.85), calls=%async_computation | async-start | bytes 262144 | tf_op jit(solution)/shard_map/all_to_all | solution.py:260
  13.5 22.1 %all-to-all-start.1 = ((bf16[8,32,2048]{2,1,0:T(8,128)(2,1)}), bf16[8,32,2048]{2,1,0:T(8,128)(2,1)S(1)}, u32[]{:S(2)}, u32[]{:S(2)}) async-start(bf16[8,32,2048]{2,1,0:T(8,128)(2,1)} %shard_map.84), calls=%async_computation.1 | async-start | bytes 2097152 | tf_op jit(solution)/shard_map/all_to_all | solution.py:260
  18.3 14.9 %collective-permute-start.1 = (bf16[256,256]{1,0:T(8,128)(2,1)S(1)}, bf16[256,256]{1,0:T(8,128)(2,1)S(1)}, u32[]{:S(2)}, u32[]{:S(2)}) collective-permute-start(bf16[256,256]{1,0:T(8,128)(2,1)S(1)} %bitcast.3), channel_id=1, source_target_pairs={{0,32},{8,40},{16,48},{24,56},{32,64},{40,72},{48,80},{56,88},{64,... | collective-permute-start | bytes 393224 | tf_op jit(solution)/shard_map/ppermute | solution.py:252
  23.5 10.9 %collective-permute-start = (bf16[256,256]{1,0:T(8,128)(2,1)S(1)}, bf16[256,256]{1,0:T(8,128)(2,1)S(1)}, u32[]{:S(2)}, u32[]{:S(2)}) collective-permute-start(bf16[256,256]{1,0:T(8,128)(2,1)S(1)} %bitcast.4), channel_id=1, source_target_pairs={{0,16},{8,24},{16,32},{24,40},{32,48},{40,56},{48,64},{56,72},{64,... | collective-permute-start | bytes 393224 | tf_op jit(solution)/shard_map/ppermute | solution.py:252
  33.2 2.4 %copy-start = (s32[16]{0:T(128)S(1)}, s32[16]{0:T(128)}, u32[]{:S(2)}) copy-start(s32[16]{0:T(128)} %doc_ref.1) | copy-start | bytes 196
  33.2 1.4 %collective-permute-start.3 = (bf16[256,256]{1,0:T(8,128)(2,1)S(1)}, bf16[256,256]{1,0:T(8,128)(2,1)S(1)}, u32[]{:S(2)}, u32[]{:S(2)}) collective-permute-start(bf16[256,256]{1,0:T(8,128)(2,1)S(1)} %broadcast_select_fusion), channel_id=1, source_target_pairs={{0,8},{8,0},{16,24},{24,16},{32,40},{40,32},{48,56},{56,48},{64,72... | collective-permute-start | bytes 393224 | tf_op jit(solution)/shard_map/ppermute | solution.py:256
  34.3 1.3 %collective-permute-start.2 = (bf16[256,256]{1,0:T(8,128)(2,1)S(1)}, bf16[256,256]{1,0:T(8,128)(2,1)S(1)}, u32[]{:S(2)}, u32[]{:S(2)}) collective-permute-start(bf16[256,256]{1,0:T(8,128)(2,1)S(1)} %collective-permute-done.two_ref), channel_id=1, source_target_pairs={{0,8},{8,0},{16,24},{24,16},{32,40},{40,32},{48,56},{56,48},{64,72... | collective-permute-start | bytes 393224 | tf_op jit(solution)/shard_map/ppermute | solution.py:256
  43.9 1.5 %collective-permute-start.4 = (bf16[256,512]{1,0:T(8,128)(2,1)S(1)}, bf16[256,512]{1,0:T(8,128)(2,1)S(1)}, u32[]{:S(2)}, u32[]{:S(2)}) collective-permute-start(bf16[256,512]{1,0:T(8,128)(2,1)S(1)} %get-tuple-element.15), channel_id=1, source_target_pairs={{0,8},{8,0},{16,24},{24,16},{32,40},{40,32},{48,56},{56,48},{64,72... | collective-permute-start | bytes 786440 | tf_op jit(solution)/shard_map/ppermute | solution.py:256
  45.6 10.5 %collective-permute-start.5 = (bf16[256,256]{1,0:T(8,128)(2,1)S(1)}, bf16[256,256]{1,0:T(8,128)(2,1)S(1)}, u32[]{:S(2)}, u32[]{:S(2)}) collective-permute-start(bf16[256,256]{1,0:T(8,128)(2,1)S(1)} %get-tuple-element.17), channel_id=1, source_target_pairs={{32,0},{40,8},{48,16},{56,24},{64,32},{72,40},{80,48},{88,56},{96,... | collective-permute-start | bytes 393224 | tf_op jit(solution)/shard_map/ppermute | solution.py:252
  52.3 7.2 %collective-permute-start.6 = (bf16[256,256]{1,0:T(8,128)(2,1)S(1)}, bf16[256,256]{1,0:T(8,128)(2,1)S(1)}, u32[]{:S(2)}, u32[]{:S(2)}) collective-permute-start(bf16[256,256]{1,0:T(8,128)(2,1)S(1)} %get-tuple-element.16), channel_id=1, source_target_pairs={{16,0},{24,8},{32,16},{40,24},{48,32},{56,40},{64,48},{72,56},{80,... | collective-permute-start | bytes 393224 | tf_op jit(solution)/shard_map/ppermute | solution.py:252
